TPU v7x, 512 devices: a whole 4x4x16 slice. The times are simulated.
512 devices in a mesh: lon: 16 (over y, x_lo, core), lat: 32 (over z, x_hi).
Axes of the slice: x: 4 (x_hi: 2, x_lo: 2; x = x_hi * 2 + x_lo), y: 4, z: 16, core: 2. Of those that a mesh axis runs over, the one named last changes fastest.
Arguments:
- field: bfloat16 [256, 2048, 256], P('lat', 'lon'), may hold values from -6 to 6
- conv_weight: bfloat16 [3, 3, 256, 256], replicated, may hold values from -0.125 to 0.125
- query_weight: bfloat16 [256, 1024], replicated, may hold values from -3.6 to 3.6
- key_weight: bfloat16 [256, 1024], replicated, may hold values from -0.6 to 0.6
- value_weight: bfloat16 [256, 1024], replicated, may hold values from -0.375 to 0.375
- query_rows: int32 [32, 16, 1], P('lat', 'lon'), may hold values from 0 to 1, as said below
- attended_grad: bfloat16 [32, 512, 1024], P('lat', 'lon'), may hold values from -6 to 6
Outputs:
- attended: bfloat16 [32, 512, 1024], P('lat', 'lon')
- field_grad: bfloat16 [256, 2048, 256], P('lat', 'lon')
Inputs may be any that keep to these rules, and one draw needn't show every extreme that they name: `query_rows`: within one block the 1 entries are distinct and increasing.
All inputs are finite; a program needn't handle non-finite values.
Results may differ from a plain program's by a relative error of at most 0.033.
Values may be sent and summed in bfloat16 or wider, within the bound.
A program may use at most 128 MiB of HBM per device.

v0:
```python
import jax
import jax.numpy as jnp
from jax import lax
from jax.sharding import PartitionSpec as P

HEAD_DIM = 64


norm_eps = 1e-05


def with_halo(cells, sides, width):
    for axis, dim in sides:
        count = lax.axis_size(axis)
        head = lax.slice_in_dim(cells, 0, width, axis=dim)
        tail = lax.slice_in_dim(cells, cells.shape[dim] - width, cells.shape[dim], axis=dim)
        cells = jnp.concatenate(
            [
                lax.ppermute(tail, axis, [(i, (i + 1) % count) for i in range(count)]),
                cells,
                lax.ppermute(head, axis, [((i + 1) % count, i) for i in range(count)]),
            ],
            axis=dim,
        )
    return cells


def open_poles(padded, lat_rows):
    lat_index = lax.axis_index("lat")
    last_band = lax.axis_size("lat") - 1
    row_ids = lax.broadcasted_iota(jnp.int32, (lat_rows + 2, 1, 1), 0)
    at_pole = (row_ids == 0) & (lat_index == 0) | (row_ids == lat_rows + 1) & (
        lat_index == last_band
    )
    return jnp.where(at_pole, jnp.zeros_like(padded), padded)


def convolve(padded, kernel, lat_rows, lon_cols):
    summed = jnp.zeros((lat_rows * lon_cols, kernel.shape[3]), jnp.float32)
    for tap_row in range(3):
        for tap_col in range(3):
            window = padded[tap_row : tap_row + lat_rows, tap_col : tap_col + lon_cols].reshape(
                lat_rows * lon_cols, -1
            )
            summed = summed + jnp.dot(
                window, kernel[tap_row, tap_col], preferred_element_type=jnp.float32
            )
    return summed.reshape(lat_rows, lon_cols, -1)


def on_device(
    field, conv_weight, query_weight, key_weight, value_weight, query_rows, attended_grad
):
    lat_rows, lon_cols, channels = field.shape
    pool_rows, pool_cols = (lat_rows // 4, lon_cols // 4)
    attn_width = key_weight.shape[1]
    head_count = attn_width // HEAD_DIM
    query_sel = query_rows.shape[2]
    query_count = query_sel * pool_cols
    key_count = pool_rows * pool_cols
    score_scale = HEAD_DIM ** (-0.5)
    padded = with_halo(field, (("lon", 1), ("lat", 0)), 1)
    conv_out = convolve(open_poles(padded, lat_rows), conv_weight, lat_rows, lon_cols)
    pooled = jax.nn.silu(conv_out).reshape(pool_rows, 4, pool_cols, 4, channels).mean(axis=(1, 3))
    centred = pooled - pooled.mean(-1, keepdims=True)
    inv_std = lax.rsqrt((centred * centred).mean(-1, keepdims=True) + norm_eps)
    standard = centred * inv_std
    normed = standard.astype(jnp.bfloat16)
    flat_normed = normed.reshape(key_count, channels)
    onehot = (
        query_rows[0, 0][:, None] == lax.broadcasted_iota(jnp.int32, (1, pool_rows), 1)
    ).astype(jnp.bfloat16)
    selected = jnp.einsum("qr,rsc->qsc", onehot, normed, preferred_element_type=jnp.float32).astype(
        jnp.bfloat16
    )
    queries = jnp.dot(
        selected.reshape(query_count, channels), query_weight, preferred_element_type=jnp.float32
    ).astype(jnp.bfloat16)
    key_rows = jnp.dot(flat_normed, key_weight, preferred_element_type=jnp.float32).astype(
        jnp.bfloat16
    )
    value_rows = jnp.dot(flat_normed, value_weight, preferred_element_type=jnp.float32).astype(
        jnp.bfloat16
    )
    band_keys, band_values = (
        lax.all_gather(key_rows, "lon", axis=0, tiled=True),
        lax.all_gather(value_rows, "lon", axis=0, tiled=True),
    )
    band_total = band_keys.shape[0]
    query_heads = queries.reshape(query_count, head_count, HEAD_DIM)
    key_heads = band_keys.reshape(band_total, head_count, HEAD_DIM)
    value_heads = band_values.reshape(band_total, head_count, HEAD_DIM)
    scores = (
        jnp.einsum("qhd,khd->hqk", query_heads, key_heads, preferred_element_type=jnp.float32)
        * score_scale
    )
    row_max = scores.max(-1, keepdims=True)
    expo_terms = jnp.exp(scores - row_max)
    exp_sum = expo_terms.sum(-1, keepdims=True)
    attn_probs = expo_terms / exp_sum
    probs_low = attn_probs.astype(jnp.bfloat16)
    attn_out = jnp.einsum(
        "hqk,khd->qhd", probs_low, value_heads, preferred_element_type=jnp.float32
    )
    attended = attn_out.astype(jnp.bfloat16).reshape(query_sel, pool_cols, attn_width)
    grad_heads = attended_grad.reshape(query_count, head_count, HEAD_DIM)
    dprob = jnp.einsum("qhd,khd->hqk", grad_heads, value_heads, preferred_element_type=jnp.float32)
    row_delta = jnp.einsum("qhd,qhd->hq", grad_heads.astype(jnp.float32), attn_out)
    score_grad = (attn_probs * (dprob - row_delta[:, :, None]) * score_scale).astype(jnp.bfloat16)
    query_grad = jnp.einsum(
        "hqk,khd->qhd", score_grad, key_heads, preferred_element_type=jnp.float32
    ).astype(jnp.bfloat16)
    query_feat = jnp.einsum(
        "qa,ca->qc",
        query_grad.reshape(query_count, attn_width),
        query_weight,
        preferred_element_type=jnp.float32,
    )
    key_part = jnp.einsum(
        "hqk,qhd->khd", score_grad, query_heads, preferred_element_type=jnp.float32
    ).astype(jnp.bfloat16)
    value_part = jnp.einsum(
        "hqk,qhd->khd", probs_low, grad_heads, preferred_element_type=jnp.float32
    ).astype(jnp.bfloat16)
    feat_term = jnp.einsum(
        "ka,ca->kc",
        key_part.reshape(key_count * lax.axis_size("lon"), attn_width),
        key_weight,
        preferred_element_type=jnp.float32,
    )
    key_feat = lax.psum_scatter(
        (
            feat_term
            + jnp.einsum(
                "ka,ca->kc",
                value_part.reshape(key_count * lax.axis_size("lon"), attn_width),
                value_weight,
                preferred_element_type=jnp.float32,
            )
        ).astype(jnp.bfloat16),
        "lon",
        scatter_dimension=0,
        tiled=True,
    ).astype(jnp.float32)
    placed = jnp.einsum(
        "qr,qsc->rsc",
        onehot.astype(jnp.float32),
        query_feat.reshape(query_sel, pool_cols, channels),
    )
    normed_grad = key_feat.reshape(pool_rows, pool_cols, channels) + placed
    pooled_grad = inv_std * (
        normed_grad
        - normed_grad.mean(-1, keepdims=True)
        - standard * (normed_grad * standard).mean(-1, keepdims=True)
    )
    spread_grad = jnp.broadcast_to(
        (pooled_grad / 16.0)[:, None, :, None, :], (pool_rows, 4, pool_cols, 4, channels)
    ).reshape(lat_rows, lon_cols, channels)
    sigmoid_out = jax.nn.sigmoid(conv_out)
    conv_grad = (spread_grad * (sigmoid_out * (1.0 + conv_out * (1.0 - sigmoid_out)))).astype(
        jnp.bfloat16
    )
    padded_grad = with_halo(conv_grad, (("lon", 1), ("lat", 0)), 1)
    flipped = jnp.swapaxes(conv_weight[::-1, ::-1], 2, 3)
    field_grad = convolve(open_poles(padded_grad, lat_rows), flipped, lat_rows, lon_cols).astype(
        jnp.bfloat16
    )
    return (attended, field_grad)


def solution(mesh):
    return jax.shard_map(
        on_device,
        mesh=mesh,
        in_specs=(
            P("lat", "lon", None),
            P(),
            P(),
            P(),
            P(),
            P("lat", "lon", None),
            P("lat", "lon", None),
        ),
        out_specs=(P("lat", "lon", None), P("lat", "lon", None)),
        check_vma=False,
    )
```

profile of v0, /device:TPU:1, one launch (start us, length us, event | category | flops | bytes accessed | tf_op | source)
XLA Modules:
  0.0 257.0 jit_solution(4539062898511247458)
XLA Ops:
  8.1 8.8 %collective-permute-start.1 = (bf16[8,1,256]{2,1,0:T(2,128)(2,1)S(1)}, bf16[8,1,256]{2,1,0:T(2,128)(2,1)S(1)}, u32[]{:S(2)}, u32[]{:S(2)}) collective-permute-start(bf16[8,1,256]{2,1,0:T(2,128)(2,1)S(1)} %get-tuple-element.29), channel_id=1, source_target_pairs={{32,0},{64,32},{96,64},{128,96},{160,128},{192,160},{224,192},{256... | collective-permute-start | bytes 12296 | tf_op jit(solution)/shard_map/ppermute | solution.py:21
  16.9 1.9 collective-permute-start
  20.8 10.8 %collective-permute-start.3 = (bf16[1,130,256]{2,1,0:T(8,128)(2,1)S(1)}, bf16[1,130,256]{2,1,0:T(8,128)(2,1)S(1)}, u32[]{:S(2)}, u32[]{:S(2)}) collective-permute-start(bf16[1,130,256]{2,1,0:T(8,128)(2,1)S(1)} %get-tuple-element.25), channel_id=1, source_target_pairs={{1,0},{2,1},{3,2},{4,3},{5,4},{6,5},{7,6},{8,7},{9,8},{10,9},{11,1... | collective-permute-start | bytes 199688 | tf_op jit(solution)/shard_map/ppermute | solution.py:21
  31.7 1.9 collective-permute-start.2
  33.6 6.7 %collective-permute-done.2 = bf16[1,130,256]{2,1,0:T(8,128)(2,1)S(1)} collective-permute-done((bf16[1,130,256]{2,1,0:T(8,128)(2,1)S(1)}, bf16[1,130,256]{2,1,0:T(8,128)(2,1)S(1)}, u32[]{:S(2)}, u32[]{:S(2)}) %collective-permute-start.2) | collective-permute-done | bytes 66592 | tf_op jit(solution)/shard_map/ppermute | solution.py:19
  48.3 1.9 convolution_convert_fusion.3
  51.8 33.8 %all-gather.5.cloned.1.call-done = bf16[1024,1024]{1,0:T(8,128)(2,1)} async-done(((bf16[64,1024]{1,0:T(8,128)(2,1)}), bf16[1024,1024]{1,0:T(8,128)(2,1)}) %all-gather.5.cloned.1.call-update) | async-done | bytes 2097168 | tf_op jit(solution)/shard_map/all_gather | solution.py:86
  85.6 2.9 %copy.18 = bf16[1024,1024]{0,1:T(8,128)(2,1)S(1)} copy(bf16[1024,1024]{1,0:T(8,128)(2,1)} %all-gather.5.cloned.1.call-done) | data formatting | bytes 4194304 | tf_op jit(solution)/shard_map/all_gather | solution.py:86
  90.3 1.8 fusion.62
  92.1 38.0 %all-gather.3.cloned.1.call-done = bf16[1024,1024]{1,0:T(8,128)(2,1)} async-done(((bf16[64,1024]{1,0:T(8,128)(2,1)}), bf16[1024,1024]{1,0:T(8,128)(2,1)}) %all-gather.3.cloned.1.call-update) | async-done | bytes 2097168 | tf_op jit(solution)/shard_map/all_gather | solution.py:87
  130.1 3.9 %copy.17 = bf16[1024,1024]{0,1:T(8,128)(2,1)} copy(bf16[1024,1024]{1,0:T(8,128)(2,1)} %all-gather.3.cloned.1.call-done) | data formatting | bytes 4194304 | tf_op jit(solution)/shard_map/all_gather | solution.py:87
  134.0 4.0 %bitcast_convert_fusion = (bf16[32,16,64]{2,0,1:T(8,128)(2,1)}, f32[16,64,32]{1,2,0:T(8,128)}) fusion(bf16[1024,16,64]{0,2,1:T(8,128)(2,1)} %bitcast.158, f32[16,32]{1,0:T(8,128)S(1)} %get-tuple-element.32, f32[16,32,1024]{2,1,0:T(8,128)} %copy-done.3), kind=kOutput, calls=%fused_computation.42 | convolution fusion | flops 69240320 | bytes 4392960 | tf_op jit(solution)/shard_map/hqk,khd->qhd/dot_general | solution.py:102
  138.0 4.1 %convolution_convert_fusion = bf16[16,1024,64]{1,2,0:T(8,128)(2,1)} fusion(bf16[32,16,64]{2,1,0:T(8,128)(2,1)S(1)} %reshape.190, f32[16,32]{1,0:T(8,128)S(1)} %get-tuple-element.32, f32[16,32,1024]{2,1,0:T(8,128)} %copy-done.3), kind=kOutput, calls=%fused_computation.7 | convolution fusion | flops 70256128 | bytes 4261888 | tf_op jit(solution)/shard_map/hqk,qhd->khd/dot_general | solution.py:122
  143.3 2.8 %fusion.2 = bf16[16,32,1024]{2,1,0:T(8,128)(2,1)S(1)} fusion(bf16[1024,16,64]{0,2,1:T(8,128)(2,1)} %bitcast.159, f32[16,32]{1,0:T(8,128)S(1)} %copy.33, f32[16,32,1024]{2,1,0:T(8,128)} %get-tuple-element.33, f32[16,32]{1,0:T(8,128)S(1)} %get-tuple-element.32, bf16[32,16,64]{2,1,0:T(8,128)(2,1)S(1)} %reshape.190), kind=kOutput, calls=%fused_computation.3 | convolution fusion | flops 69730304 | bytes 5312512 | tf_op jit(solution)/shard_map/qhd,khd->hqk/dot_general | solution.py:107
  148.7 1.6 fusion.4
  150.2 1.9 fusion.6
  152.6 63.3 %reduce-scatter.2.cloned.1.call-done = bf16[64,256]{1,0:T(8,128)(2,1)} async-done(((bf16[1024,256]{1,0:T(8,128)(2,1)}), bf16[64,256]{1,0:T(8,128)(2,1)}) %reduce-scatter.2.cloned.1.call-update) | async-done | bytes 32784 | tf_op jit(solution)/shard_map/reduce_scatter | solution.py:131
  218.9 1.6 reshape.196
  220.9 5.0 %collective-permute-start.5 = (bf16[8,1,256]{2,1,0:T(2,128)(2,1)S(1)}, bf16[8,1,256]{2,1,0:T(2,128)(2,1)S(1)}, u32[]{:S(2)}, u32[]{:S(2)}) collective-permute-start(bf16[8,1,256]{2,1,0:T(2,128)(2,1)S(1)} %get-tuple-element.27), channel_id=1, source_target_pairs={{32,0},{64,32},{96,64},{128,96},{160,128},{192,160},{224,192},{256... | collective-permute-start | bytes 12296 | tf_op jit(solution)/shard_map/ppermute | solution.py:21
  225.9 1.9 collective-permute-start.4
  227.9 2.1 collective-permute-done.4
  230.0 7.0 %collective-permute-start.7 = (bf16[1,130,256]{2,1,0:T(8,128)(2,1)S(1)}, bf16[1,130,256]{2,1,0:T(8,128)(2,1)S(1)}, u32[]{:S(2)}, u32[]{:S(2)}) collective-permute-start(bf16[1,130,256]{2,1,0:T(8,128)(2,1)S(1)} %get-tuple-element.23), channel_id=1, source_target_pairs={{1,0},{2,1},{3,2},{4,3},{5,4},{6,5},{7,6},{8,7},{9,8},{10,9},{11,1... | collective-permute-start | bytes 199688 | tf_op jit(solution)/shard_map/ppermute | solution.py:21
  237.0 1.9 collective-permute-start.6
  239.9 5.8 %collective-permute-done.6 = bf16[1,130,256]{2,1,0:T(8,128)(2,1)S(1)} collective-permute-done((bf16[1,130,256]{2,1,0:T(8,128)(2,1)S(1)}, bf16[1,130,256]{2,1,0:T(8,128)(2,1)S(1)}, u32[]{:S(2)}, u32[]{:S(2)}) %collective-permute-start.6) | collective-permute-done | bytes 66592 | tf_op jit(solution)/shard_map/ppermute | solution.py:19
  (94 shorter events, 26.6 us)
Async XLA Ops:
  7.2 40.2 %copy-start = (bf16[256,1024]{1,0:T(8,128)(2,1)S(1)}, bf16[256,1024]{1,0:T(8,128)(2,1)}, u32[]{:S(2)}) copy-start(bf16[256,1024]{1,0:T(8,128)(2,1)} %param.10) | copy-start | bytes 1572868
  7.2 78.4 %all-gather.5.cloned.1.call-start = ((), (), s32[]{:S(2)}) async-start(), calls=%async_computation.2 | async-start | bytes 2228224 | tf_op jit(solution)/shard_map/all_gather | solution.py:86
  8.1 10.7 %collective-permute-start.1 = (bf16[8,1,256]{2,1,0:T(2,128)(2,1)S(1)}, bf16[8,1,256]{2,1,0:T(2,128)(2,1)S(1)}, u32[]{:S(2)}, u32[]{:S(2)}) collective-permute-start(bf16[8,1,256]{2,1,0:T(2,128)(2,1)S(1)} %get-tuple-element.29), channel_id=1, source_target_pairs={{32,0},{64,32},{96,64},{128,96},{160,128},{192,160},{224,192},{256... | collective-permute-start | bytes 12296 | tf_op jit(solution)/shard_map/ppermute | solution.py:21
  16.9 3.1 %collective-permute-start = (bf16[8,1,256]{2,1,0:T(2,128)(2,1)S(1)}, bf16[8,1,256]{2,1,0:T(2,128)(2,1)S(1)}, u32[]{:S(2)}, u32[]{:S(2)}) collective-permute-start(bf16[8,1,256]{2,1,0:T(2,128)(2,1)S(1)} %get-tuple-element.28), channel_id=1, source_target_pairs={{0,32},{32,64},{64,96},{96,128},{128,160},{160,192},{192,224},{224... | collective-permute-start | bytes 12296 | tf_op jit(solution)/shard_map/ppermute | solution.py:19
  20.8 12.8 %collective-permute-start.3 = (bf16[1,130,256]{2,1,0:T(8,128)(2,1)S(1)}, bf16[1,130,256]{2,1,0:T(8,128)(2,1)S(1)}, u32[]{:S(2)}, u32[]{:S(2)}) collective-permute-start(bf16[1,130,256]{2,1,0:T(8,128)(2,1)S(1)} %get-tuple-element.25), channel_id=1, source_target_pairs={{1,0},{2,1},{3,2},{4,3},{5,4},{6,5},{7,6},{8,7},{9,8},{10,9},{11,1... | collective-permute-start | bytes 199688 | tf_op jit(solution)/shard_map/ppermute | solution.py:21
  31.7 8.7 %collective-permute-start.2 = (bf16[1,130,256]{2,1,0:T(8,128)(2,1)S(1)}, bf16[1,130,256]{2,1,0:T(8,128)(2,1)S(1)}, u32[]{:S(2)}, u32[]{:S(2)}) collective-permute-start(bf16[1,130,256]{2,1,0:T(8,128)(2,1)S(1)} %get-tuple-element.24), channel_id=1, source_target_pairs={{0,1},{1,2},{2,3},{3,4},{4,5},{5,6},{6,7},{7,8},{8,9},{9,10},{10,1... | collective-permute-start | bytes 199688 | tf_op jit(solution)/shard_map/ppermute | solution.py:19
  41.7 1.3 copy-start.4
  45.7 2.5 copy-start.1
  46.0 5.1 %copy-start.10 = (bf16[1,32,1024]{2,1,0:T(8,128)(2,1)S(1)}, bf16[1,32,1024]{2,1,0:T(8,128)(2,1)}, u32[]{:S(2)}) copy-start(bf16[1,32,1024]{2,1,0:T(8,128)(2,1)} %param.13) | copy-start | bytes 196612
  46.0 5.4 %copy-start.7 = (bf16[256,1024]{1,0:T(8,128)(2,1)S(1)}, bf16[256,1024]{1,0:T(8,128)(2,1)}, u32[]{:S(2)}) copy-start(bf16[256,1024]{1,0:T(8,128)(2,1)} %param.9) | copy-start | bytes 1572868
  48.2 81.8 %all-gather.3.cloned.1.call-start = ((), (), s32[]{:S(2)}) async-start(), calls=%async_computation.1 | async-start | bytes 2228224 | tf_op jit(solution)/shard_map/all_gather | solution.py:87
  50.2 165.7 %reduce-scatter.2.cloned.1.call-start = ((), (), s32[]{:S(2)}) async-start(), calls=%async_computation.3 | async-start | bytes 557056 | tf_op jit(solution)/shard_map/reduce_scatter | solution.py:131
  88.9 1.4 copy-start.3
  146.1 1.6 copy-start.6
  146.9 1.0 copy-start.8
  146.9 1.8 copy-start.11
  152.4 68.1 %copy-start.2 = (f32[1024,256]{1,0:T(8,128)S(1)}, f32[1024,256]{1,0:T(8,128)}, u32[]{:S(2)}) copy-start(f32[1024,256]{1,0:T(8,128)} %copy-done.1) | copy-start | bytes 3145732
  220.4 18.5 %copy-start.5 = (bf16[3,3,256,256]{3,2,1,0:T(8,128)(2,1)S(1)}, bf16[3,3,256,256]{3,2,1,0:T(8,128)(2,1)}, u32[]{:S(2)}) copy-start(bf16[3,3,256,256]{3,2,1,0:T(8,128)(2,1)} %param.8) | copy-start | bytes 3538948
  220.9 18.2 %copy-start.9 = (bf16[32,16,64]{2,0,1:T(8,128)(2,1)S(1)}, bf16[32,16,64]{2,0,1:T(8,128)(2,1)}, u32[]{:S(2)}) copy-start(bf16[32,16,64]{2,0,1:T(8,128)(2,1)} %get-tuple-element.34) | copy-start | bytes 196612
  220.9 7.0 %collective-permute-start.5 = (bf16[8,1,256]{2,1,0:T(2,128)(2,1)S(1)}, bf16[8,1,256]{2,1,0:T(2,128)(2,1)S(1)}, u32[]{:S(2)}, u32[]{:S(2)}) collective-permute-start(bf16[8,1,256]{2,1,0:T(2,128)(2,1)S(1)} %get-tuple-element.27), channel_id=1, source_target_pairs={{32,0},{64,32},{96,64},{128,96},{160,128},{192,160},{224,192},{256... | collective-permute-start | bytes 12296 | tf_op jit(solution)/shard_map/ppermute | solution.py:21
  225.9 4.0 %collective-permute-start.4 = (bf16[8,1,256]{2,1,0:T(2,128)(2,1)S(1)}, bf16[8,1,256]{2,1,0:T(2,128)(2,1)S(1)}, u32[]{:S(2)}, u32[]{:S(2)}) collective-permute-start(bf16[8,1,256]{2,1,0:T(2,128)(2,1)S(1)} %get-tuple-element.26), channel_id=1, source_target_pairs={{0,32},{32,64},{64,96},{96,128},{128,160},{160,192},{192,224},{224... | collective-permute-start | bytes 12296 | tf_op jit(solution)/shard_map/ppermute | solution.py:19
  230.0 9.9 %collective-permute-start.7 = (bf16[1,130,256]{2,1,0:T(8,128)(2,1)S(1)}, bf16[1,130,256]{2,1,0:T(8,128)(2,1)S(1)}, u32[]{:S(2)}, u32[]{:S(2)}) collective-permute-start(bf16[1,130,256]{2,1,0:T(8,128)(2,1)S(1)} %get-tuple-element.23), channel_id=1, source_target_pairs={{1,0},{2,1},{3,2},{4,3},{5,4},{6,5},{7,6},{8,7},{9,8},{10,9},{11,1... | collective-permute-start | bytes 199688 | tf_op jit(solution)/shard_map/ppermute | solution.py:21
  237.0 8.7 %collective-permute-start.6 = (bf16[1,130,256]{2,1,0:T(8,128)(2,1)S(1)}, bf16[1,130,256]{2,1,0:T(8,128)(2,1)S(1)}, u32[]{:S(2)}, u32[]{:S(2)}) collective-permute-start(bf16[1,130,256]{2,1,0:T(8,128)(2,1)S(1)} %get-tuple-element.22), channel_id=1, source_target_pairs={{0,1},{1,2},{2,3},{3,4},{4,5},{5,6},{6,7},{7,8},{8,9},{9,10},{10,1... | collective-permute-start | bytes 199688 | tf_op jit(solution)/shard_map/ppermute | solution.py:19
Sparse Core Ops, SparseCore 0:
  48.4 37.2 all-gather.4
  88.3 41.7 all-gather.2
  150.4 65.5 reduce-scatter.1
where the time goes:
time: 258 us; the launch traced here: 257 us
  waiting for transfers between devices  151 us (59%)
  starting transfers between devices  39.6 us (15%)
  matrix products  26 us (10%)
  local copies, waits for them, and re-layouts  16.5 us (6%)
  between operations  14.9 us (6%)
  other arithmetic  9.01 us (3%)
    reduce_scatter x1, waiting for transfers between devices, on_device(): lax.psum_scatter((feat_term + jnp.einsum('ka,ca->kc', value_part.reshape(...  63.3 us
    all_gather x1, waiting for transfers between devices, on_device(): lax.all_gather(value_rows, 'lon', axis=0, tiled=True)  38 us
    all_gather x1, waiting for transfers between devices, on_device(): lax.all_gather(key_rows, 'lon', axis=0, tiled=True)  33.8 us
    ppermute x4, starting transfers between devices, with_halo(): lax.ppermute(head, axis, [((i + 1) % count, i) for i in range(count)])  31.7 us
    ppermute x4, waiting for transfers between devices, with_halo(): lax.ppermute(tail, axis, [(i, (i + 1) % count) for i in range(count)])  15.7 us
    ppermute x4, starting transfers between devices, with_halo(): lax.ppermute(tail, axis, [(i, (i + 1) % count) for i in range(count)])  7.68 us
    dot_general x18, matrix products, convolve(): jnp.dot(window, kernel[tap_row, tap_col], preferred_element_type=jnp.floa...  6.43 us
  transfers between devices with their start and end apart: 11, of which 7 were waited for; matrix products, arithmetic and copies ran while one was open for 4% of the time, Pallas kernels for 0%

commit v1 on v0

v1 whole, which is shorter than its diff:
```python
import jax
import jax.numpy as jnp
from jax import lax
from jax.experimental import pallas as pl
from jax.experimental.pallas import tpu as pltpu
from jax.sharding import PartitionSpec as P

HEAD_DIM = 64
NORM_EPS = 1e-05
POOL = 4
BF16 = jnp.bfloat16
F32 = jnp.float32

NN = (((1,), (0,)), ((), ()))
NT = (((1,), (1,)), ((), ()))


def mm(a, b, dims=NN):
    return lax.dot_general(a, b, dims, preferred_element_type=F32)


def eye(n):
    rows = lax.broadcasted_iota(jnp.int32, (n, n), 0)
    cols = lax.broadcasted_iota(jnp.int32, (n, n), 1)
    return jnp.where(rows == cols, 1.0, 0.0).astype(BF16)


def make_kernel(lon_n, lat_n, rows, cols, chan, width):
    pr, ps = rows // POOL, cols // POOL
    keys = pr * ps
    heads = width // HEAD_DIM
    hq = heads * ps
    group = chan // HEAD_DIM
    groups = heads // group
    gq = group * ps
    slab_rows = (POOL + 2) * ps
    halo = [
        (0, 0, 1, 0), (1, 0, -1, 0),
        (0, 1, 1, 1), (1, 1, -1, 1),
        (0, 2, 1, -1), (1, 2, -1, -1),
    ]

    def kernel(
        field, conv_w, wq_h, wk_h, wv_h, qrow, ag_h,
        attended, out_grad,
        xr, xs, cg, cw, cwt, wq, wk, wv, ag,
        cout, dsl, nall, ntr, pt, qg, part, recv,
        colmsg, colhalo, obuf, abuf,
        load_sem, out_sem, halo_send, halo_recv, row_send, row_recv,
        g_send, g_recv, s_send, s_recv,
    ):
        lon = lax.axis_index("lon")
        lat = lax.axis_index("lat")

        def at(dlon, dlat):
            return {
                "lon": lax.rem(lon + dlon + lon_n, lon_n),
                "lat": lax.rem(lat + dlat + lat_n, lat_n),
            }

        loads = [
            pltpu.make_async_copy(field, xr.at[pl.ds(1, rows)], load_sem.at[0]),
            pltpu.make_async_copy(conv_w, cw, load_sem.at[1]),
            pltpu.make_async_copy(ag_h.at[0], ag, load_sem.at[2]),
            pltpu.make_async_copy(wv_h, wv, load_sem.at[3]),
            pltpu.make_async_copy(wq_h, wq, load_sem.at[4]),
            pltpu.make_async_copy(wk_h, wk, load_sem.at[5]),
        ]
        for load in loads:
            load.start()

        barrier = pltpu.get_barrier_semaphore()

        def greet(d, _):
            pl.semaphore_signal(
                barrier, inc=1, device_id=at(d, 0), device_id_type=pl.DeviceIdType.MESH
            )
            return 0

        lax.fori_loop(1, lon_n, greet, 0)
        for dlat in (-1, 1):
            for dlon in (-1, 0, 1):
                pl.semaphore_signal(
                    barrier, inc=1, device_id=at(dlon, dlat), device_id_type=pl.DeviceIdType.MESH
                )

        def column_copies(phase):
            return [
                pltpu.make_async_remote_copy(
                    src_ref=colmsg.at[phase, side],
                    dst_ref=colhalo.at[phase, side, place],
                    send_sem=halo_send.at[phase, k],
                    recv_sem=halo_recv.at[phase, k],
                    device_id=at(dlon, dlat),
                    device_id_type=pl.DeviceIdType.MESH,
                )
                for k, (side, place, dlon, dlat) in enumerate(halo)
            ]

        def row_copies(phase, up_src, up_dst, down_src, down_dst):
            return [
                pltpu.make_async_remote_copy(
                    src_ref=src,
                    dst_ref=dst,
                    send_sem=row_send.at[phase, k],
                    recv_sem=row_recv.at[phase, k],
                    device_id=at(0, dlat),
                    device_id_type=pl.DeviceIdType.MESH,
                )
                for k, (src, dst, dlat) in enumerate(
                    ((up_src, up_dst, -1), (down_src, down_dst, 1))
                )
            ]

        loads[0].wait()
        for i in range(rows):
            colmsg[0, 0, i : i + 1, :] = xr[1 + i, cols - 16 : cols, :].astype(F32)[15:16]
            colmsg[0, 1, i : i + 1, :] = xr[1 + i, 0:16, :].astype(F32)[0:1]
        pl.semaphore_wait(barrier, lon_n - 1 + 6)
        cols_out = column_copies(0)
        rows_out = row_copies(0, xr.at[1], xr.at[rows + 1], xr.at[rows], xr.at[0])
        for c in rows_out + cols_out:
            c.start()

        prow = lax.broadcasted_iota(jnp.int32, (slab_rows, cols), 0)
        pcol = lax.broadcasted_iota(jnp.int32, (slab_rows, cols), 1)
        spread = jnp.where(
            pcol == (prow % ps) * POOL + prow // ps - 1, 1.0, 0.0
        ).astype(BF16)
        srow = lax.broadcasted_iota(jnp.int32, (slab_rows, chan), 0)

        def slabs(r, left, right, zero):
            y = mm(spread, xr[r])
            y = jnp.where(srow == 0, left, jnp.where(srow == slab_rows - 1, right, y))
            if zero is not None:
                y = jnp.where(zero, 0.0, y)
            xs[r] = y.astype(BF16)

        hrow = lax.broadcasted_iota(jnp.int32, (gq, chan), 0) // ps
        hcol = lax.broadcasted_iota(jnp.int32, (gq, chan), 1) // HEAD_DIM
        head_mask = hrow == hcol

        def absorb(x, w_ref, g, scale):
            part_g = x[:, g * chan : (g + 1) * chan]
            wide = jnp.where(head_mask, jnp.concatenate([part_g] * group, axis=0), 0.0)
            y = mm(wide.astype(BF16), w_ref[:, g * chan : (g + 1) * chan], NT)
            return (y * scale).astype(BF16) if scale != 1.0 else y.astype(BF16)

        loads[2].wait()
        loads[3].wait()
        for g in range(groups):
            qg[g * gq : (g + 1) * gq, :] = absorb(ag[...].astype(F32), wv, g, 1.0)

        for c in cols_out:
            c.wait()
        for i in range(rows):
            slabs(
                1 + i,
                colhalo[0, 0, 0, i : i + 1, :],
                colhalo[0, 1, 0, i : i + 1, :],
                None,
            )
        for c in rows_out:
            c.wait()
        slabs(
            0,
            colhalo[0, 0, 1, rows - 1 : rows, :],
            colhalo[0, 1, 1, rows - 1 : rows, :],
            lat == 0,
        )
        slabs(
            rows + 1,
            colhalo[0, 0, 2, 0:1, :],
            colhalo[0, 1, 2, 0:1, :],
            lat == lat_n - 1,
        )

        loads[1].wait()
        pooled = []
        for p in range(pr):
            r0 = p * POOL
            acc = None
            for a in range(3):
                lhs = jnp.concatenate(
                    [
                        xs[r0 + a : r0 + a + POOL, b * ps : b * ps + cols, :].reshape(
                            POOL * cols, chan
                        )
                        for b in range(3)
                    ],
                    axis=1,
                )
                term = mm(lhs, cw[a].reshape(3 * chan, chan))
                acc = term if acc is None else acc + term
            cout[r0 * cols : (r0 + POOL) * cols, :] = acc
            act = acc * (0.5 * jnp.tanh(0.5 * acc) + 0.5)
            pooled.append(act.reshape(POOL * POOL, ps, chan).sum(axis=0) * (1.0 / (POOL * POOL)))
        pooled = jnp.concatenate(pooled, axis=0)
        centred = pooled - pooled.mean(-1, keepdims=True)
        inv_std = lax.rsqrt((centred * centred).mean(-1, keepdims=True) + NORM_EPS)
        standard = centred * inv_std
        normed = standard.astype(BF16)
        nall[0] = normed

        def gather_copy(d):
            return pltpu.make_async_remote_copy(
                src_ref=nall.at[0],
                dst_ref=nall.at[d],
                send_sem=g_send.at[d],
                recv_sem=g_recv.at[d],
                device_id=at(d, 0),
                device_id_type=pl.DeviceIdType.MESH,
            )

        def run(fn):
            def body(d, _):
                fn(d)
                return 0

            lax.fori_loop(1, lon_n, body, 0)

        run(lambda d: gather_copy(d).start())

        first = qrow[...] == 0
        chosen = jnp.where(first, standard[:ps], standard[ps:]).astype(BF16)
        loads[4].wait()
        loads[5].wait()
        q = mm(chosen, wq[...]).astype(BF16).astype(F32)
        for g in range(groups):
            qg[hq + g * gq : hq + (g + 1) * gq, :] = absorb(q, wk, g, HEAD_DIM**-0.5)
        for i in range(rows):
            v = cout[i * cols : (i + 1) * cols, :]
            sig = 0.5 * jnp.tanh(0.5 * v) + 0.5
            dsl[i * cols : (i + 1) * cols, :] = sig * (1.0 + v * (1.0 - sig)) * (
                1.0 / (POOL * POOL)
            )
        ident = eye(chan)
        for a in range(3):
            for b in range(3):
                cwt[a, b] = mm(ident, cw[a, b], NT).astype(BF16)

        run(lambda d: gather_copy(d).wait())

        nv = nall[...].reshape(lon_n * keys, chan)
        ntr[...] = mm(ident, nv, NT).astype(BF16)
        blk = min(256, hq)
        for h0 in range(0, hq, blk):
            s = mm(nv, qg[hq + h0 : hq + h0 + blk, :], NT)
            e = jnp.exp(s - s.max(axis=0, keepdims=True))
            prob = e * (1.0 / e.sum(axis=0, keepdims=True))
            dp = mm(nv, qg[h0 : h0 + blk, :], NT)
            delta = (prob * dp).sum(axis=0, keepdims=True)
            pt[:, h0 : h0 + blk] = prob.astype(BF16)
            pt[:, hq + h0 : hq + h0 + blk] = (prob * (dp - delta)).astype(BF16)

        def scatter_copy(d):
            return pltpu.make_async_remote_copy(
                src_ref=part.at[d],
                dst_ref=recv.at[d],
                send_sem=s_send.at[d],
                recv_sem=s_recv.at[d],
                device_id=at(lon_n - d, 0),
                device_id_type=pl.DeviceIdType.MESH,
            )

        step = 4
        own = None
        for d0 in range(0, lon_n, step):
            y = mm(pt[d0 * keys : (d0 + step) * keys, :], qg[...])
            if d0 == 0:
                own = y[:keys]
            part[d0 : d0 + step] = y.astype(BF16).reshape(step, keys, chan)
            for d in range(max(d0, 1), d0 + step):
                scatter_copy(d).start()

        ident_g = eye(gq)
        qfeat = jnp.zeros((ps, chan), F32)
        for g in range(groups):
            for which in range(2):
                c0 = which * hq + g * gq
                u = mm(ntr[...], pt[:, c0 : c0 + gq]).astype(BF16)
                u = mm(ident_g, u, NT).astype(BF16)
                w = (wv, wk)[which][:, g * chan : (g + 1) * chan]
                y = jnp.where(head_mask, mm(u, w), 0.0).reshape(group, ps, chan).sum(axis=0)
                if which == 0:
                    abuf[:, g * chan : (g + 1) * chan] = y.astype(BF16)
                else:
                    y = (y * HEAD_DIM**-0.5).astype(BF16)
                    qfeat = qfeat + mm(y, wq[:, g * chan : (g + 1) * chan], NT)
        att_out = pltpu.make_async_copy(abuf, attended.at[0], out_sem.at[rows])
        att_out.start()

        zero = jnp.zeros_like(qfeat)
        total = own + jnp.concatenate(
            [jnp.where(first, qfeat, zero), jnp.where(first, zero, qfeat)], axis=0
        )
        run(lambda d: scatter_copy(d).wait())
        total = total + recv[1:].astype(F32).sum(axis=0)

        pgrad = inv_std * (
            total
            - total.mean(-1, keepdims=True)
            - standard * (total * standard).mean(-1, keepdims=True)
        )

        edge = lax.broadcasted_iota(jnp.int32, (ps, chan), 0)
        ends = {}

        def grad_row(i):
            pg = pgrad[(i // POOL) * ps : (i // POOL + 1) * ps]
            for t in range(POOL):
                at_row = i * cols + t * ps
                slab = (pg * dsl[at_row : at_row + ps, :]).astype(BF16)
                cg[1 + i, (t + 1) * ps : (t + 2) * ps, :] = slab
                if t == 0:
                    colmsg[1, 1, i : i + 1, :] = slab.astype(F32)[0:1]
                    ends[i, 0] = slab
                if t == POOL - 1:
                    colmsg[1, 0, i : i + 1, :] = slab.astype(F32)[ps - 1 : ps]
                    ends[i, 1] = slab

        mid = pl.ds(ps, cols)
        rows_out = row_copies(
            1, cg.at[1, mid], cg.at[rows + 1, mid], cg.at[rows, mid], cg.at[0, mid]
        )
        grad_row(0)
        rows_out[0].start()
        grad_row(rows - 1)
        rows_out[1].start()
        for i in range(1, rows - 1):
            grad_row(i)
        cols_out = column_copies(1)
        for c in cols_out:
            c.start()

        def edges(r, first_slab, last_slab, left, right):
            lo = pltpu.roll(last_slab.astype(F32), 1, 0)
            hi = pltpu.roll(first_slab.astype(F32), ps - 1, 0)
            cg[r, 0:ps, :] = jnp.where(edge == 0, left, lo).astype(BF16)
            cg[r, slab_rows - ps : slab_rows, :] = jnp.where(
                edge == ps - 1, right, hi
            ).astype(BF16)

        for c in cols_out:
            c.wait()
        for i in range(rows):
            edges(
                1 + i,
                ends[i, 0],
                ends[i, 1],
                colhalo[1, 0, 0, i : i + 1, :],
                colhalo[1, 1, 0, i : i + 1, :],
            )
        for c in rows_out:
            c.wait()
        for r, place, pick, pole in ((0, 1, rows - 1, 0), (rows + 1, 2, 0, lat_n - 1)):
            edges(
                r,
                cg[r, ps : 2 * ps, :],
                cg[r, POOL * ps : (POOL + 1) * ps, :],
                colhalo[1, 0, place, pick : pick + 1, :],
                colhalo[1, 1, place, pick : pick + 1, :],
            )
            cg[r] = jnp.where(lat == pole, 0.0, cg[r].astype(F32)).astype(BF16)

        prow = lax.broadcasted_iota(jnp.int32, (cols, cols), 0)
        pcol = lax.broadcasted_iota(jnp.int32, (cols, cols), 1)
        weave = jnp.where(prow == (pcol % ps) * POOL + pcol // ps, 1.0, 0.0).astype(BF16)
        stores = []
        for p in range(pr):
            r0 = p * POOL
            acc = None
            for a in range(3):
                lhs = jnp.concatenate(
                    [
                        cg[
                            r0 + 2 - a : r0 + 2 - a + POOL, (2 - b) * ps : (2 - b) * ps + cols, :
                        ].reshape(POOL * cols, chan)
                        for b in range(3)
                    ],
                    axis=1,
                )
                term = mm(lhs, cwt[a].reshape(3 * chan, chan))
                acc = term if acc is None else acc + term
            acc = acc.astype(BF16)
            for i in range(POOL):
                obuf[r0 + i] = mm(weave, acc[i * cols : (i + 1) * cols]).astype(BF16)
                store = pltpu.make_async_copy(
                    obuf.at[r0 + i], out_grad.at[r0 + i], out_sem.at[r0 + i]
                )
                store.start()
                stores.append(store)
        att_out.wait()
        for store in stores:
            store.wait()

    return kernel


def solution(mesh):
    lon_n, lat_n = mesh.shape["lon"], mesh.shape["lat"]

    def on_device(field, conv_w, wq, wk, wv, query_rows, attended_grad):
        rows, cols, chan = field.shape
        width = wq.shape[1]
        pr, ps = rows // POOL, cols // POOL
        keys = pr * ps
        hq = (width // HEAD_DIM) * ps
        slab_rows = (POOL + 2) * ps
        any_spec = pl.BlockSpec(memory_space=pl.ANY)
        vmem = pl.BlockSpec(memory_space=pltpu.VMEM)
        return pl.pallas_call(
            make_kernel(lon_n, lat_n, rows, cols, chan, width),
            out_shape=(
                jax.ShapeDtypeStruct(attended_grad.shape, BF16),
                jax.ShapeDtypeStruct(field.shape, BF16),
            ),
            in_specs=[any_spec] * 5 + [vmem, any_spec],
            out_specs=(any_spec, any_spec),
            scratch_shapes=[
                pltpu.VMEM((rows + 2, cols, chan), BF16),
                pltpu.VMEM((rows + 2, slab_rows, chan), BF16),
                pltpu.VMEM((rows + 2, slab_rows, chan), BF16),
                pltpu.VMEM((3, 3, chan, chan), BF16),
                pltpu.VMEM((3, 3, chan, chan), BF16),
                pltpu.VMEM((chan, width), BF16),
                pltpu.VMEM((chan, width), BF16),
                pltpu.VMEM((chan, width), BF16),
                pltpu.VMEM((ps, width), BF16),
                pltpu.VMEM((rows * cols, chan), F32),
                pltpu.VMEM((rows * cols, chan), F32),
                pltpu.VMEM((lon_n, keys, chan), BF16),
                pltpu.VMEM((chan, lon_n * keys), BF16),
                pltpu.VMEM((lon_n * keys, 2 * hq), BF16),
                pltpu.VMEM((2 * hq, chan), BF16),
                pltpu.VMEM((lon_n, keys, chan), BF16),
                pltpu.VMEM((lon_n, keys, chan), BF16),
                pltpu.VMEM((2, 2, rows, chan), F32),
                pltpu.VMEM((2, 2, 3, rows, chan), F32),
                pltpu.VMEM((rows, cols, chan), BF16),
                pltpu.VMEM((ps, width), BF16),
                pltpu.SemaphoreType.DMA((6,)),
                pltpu.SemaphoreType.DMA((rows + 1,)),
                pltpu.SemaphoreType.DMA((2, 6)),
                pltpu.SemaphoreType.DMA((2, 6)),
                pltpu.SemaphoreType.DMA((2, 2)),
                pltpu.SemaphoreType.DMA((2, 2)),
                pltpu.SemaphoreType.DMA((lon_n,)),
                pltpu.SemaphoreType.DMA((lon_n,)),
                pltpu.SemaphoreType.DMA((lon_n,)),
                pltpu.SemaphoreType.DMA((lon_n,)),
            ],
            compiler_params=pltpu.CompilerParams(
                collective_id=0, has_side_effects=True, vmem_limit_bytes=56 * 1024 * 1024
            ),
        )(field, conv_w, wq, wk, wv, query_rows.reshape(1, 1), attended_grad)

    return jax.shard_map(
        on_device,
        mesh=mesh,
        in_specs=(
            P("lat", "lon", None),
            P(),
            P(),
            P(),
            P(),
            P("lat", "lon", None),
            P("lat", "lon", None),
        ),
        out_specs=(P("lat", "lon", None), P("lat", "lon", None)),
        check_vma=False,
    )
```

time: 258 us -> 57.3 us (0.22)
  waiting for transfers between devices: 151 us -> 0 us
  Pallas kernels: 0 us -> 52.4 us
  starting transfers between devices: 39.6 us -> 0 us
  matrix products: 26 us -> 0 us
  between operations: 14.9 us -> 1.29 us
  local copies, waits for them, and re-layouts: 16.5 us -> 3.34 us
  other arithmetic: 9.01 us -> 0 us
    all_gather x2 -> x0, waiting for transfers between devices: 71.8 us -> none  [the longest x1 38 us: on_device(): lax.all_gather(value_rows, 'lon', axis=0, tiled=True)]
    reduce_scatter x1 -> x0, waiting for transfers between devices: 63.3 us -> none  [on_device(): lax.psum_scatter((feat_term + jnp.einsum('ka,ca->kc', value_part.reshape(...]
    pallas_call x0 -> x1, Pallas kernels: none -> 52.4 us  [on_device(): pl.pallas_call(make_kernel(lon_n, lat_n, rows, cols, chan, width), out_sh...]
    ppermute x8 -> x0, starting transfers between devices: 39.3 us -> none  [the longest x4 31.7 us: with_halo(): lax.ppermute(head, axis, [((i + 1) % count, i) for i in range(count)])]
    dot_general x31 -> x0, matrix products: 26 us -> none  [the longest x18 6.43 us: convolve(): jnp.dot(window, kernel[tap_row, tap_col], preferred_element_type=jnp.floa...]
    ppermute x8 -> x0, waiting for transfers between devices: 15.7 us -> none  [the longest x4 15.7 us: with_halo(): lax.ppermute(tail, axis, [(i, (i + 1) % count) for i in range(count)])]
    all_gather x2 -> x0, local copies, waits for them, and re-layouts: 6.78 us -> none  [the longest x1 3.92 us: on_device(): lax.all_gather(value_rows, 'lon', axis=0, tiled=True)]
    reshape x6 -> x0, local copies, waits for them, and re-layouts: 3.1 us -> none  [the longest x1 1.58 us: on_device(): spread_grad = jnp.broadcast_to((pooled_grad / 16.0)[:, None, :, None, :],...]
  transfers between devices with their start and end apart: 11 -> 0, of which waited for: 7 -> 0; matrix products, arithmetic and copies ran while one was open for 4% -> 0% of each run, Pallas kernels for 0% -> 0%
where the time goes in v1:
time: 57.3 us; the launch traced here: 57.1 us
  Pallas kernels  52.4 us (91%)
  local copies, waits for them, and re-layouts  3.34 us (6%)
  between operations  1.29 us (2%)
    pallas_call x1, Pallas kernels, on_device(): pl.pallas_call(make_kernel(lon_n, lat_n, rows, cols, chan, width), out_sh...  52.4 us
    unnamed x2, local copies, waits for them, and re-layouts  3.34 us

profile of v1, /device:TPU:1, one launch (start us, length us, event | category | flops | bytes accessed | tf_op | source)
XLA Modules:
  0.0 57.1 jit_solution(6212798522381015389)
XLA Ops:
  1.3 52.4 %shard_map.86 = (bf16[1,32,1024]{2,1,0:T(8,128)(2,1)}, bf16[8,128,256]{2,1,0:T(8,128)(2,1)}) custom-call(bf16[8,128,256]{2,1,0:T(8,128)(2,1)} %field.1, bf16[3,3,256,256]{3,2,1,0:T(8,128)(2,1)} %conv_w.1, bf16[256,1024]{1,0:T(8,128)(2,1)} %wq_h.1, bf16[256,1024]{1,0:T(8,128)(2,1)} %wk_h.1, bf16[256,1024]{1,0:T(8,128)(2,1)} %wv_h.1, s32[1,1]{1,0:T(1,128)} %bitcast.1.qrow, ...), custom_call_target="tpu_custom_call" | custom-call | tf_op jit(solution)/shard_map/pallas_call | solution.py:412
  53.7 1.5 %copy.12 = bf16[1,32,1024]{2,1,0:T(8,128)(2,1)} copy(bf16[1,32,1024]{2,1,0:T(8,128)(2,1)} %get-tuple-element.4) | data formatting | bytes 131072
  55.2 1.9 %copy.13 = bf16[8,128,256]{2,1,0:T(8,128)(2,1)} copy(bf16[8,128,256]{2,1,0:T(8,128)(2,1)} %get-tuple-element.5) | data formatting | bytes 1048576

commit v2 on v0

v2 whole, which is shorter than its diff:
```python
import itertools

import jax
import jax.numpy as jnp
from jax import lax
from jax.experimental import pallas as pl
from jax.experimental.pallas import tpu as pltpu
from jax.sharding import PartitionSpec as P

HEAD_DIM = 64
NORM_EPS = 1e-05
POOL = 4
BF16 = jnp.bfloat16
F32 = jnp.float32
MESH = pl.DeviceIdType.MESH

NN = (((1,), (0,)), ((), ()))
NT = (((1,), (1,)), ((), ()))


def mm(a, b, dims=NN):
    return lax.dot_general(a, b, dims, preferred_element_type=F32)


def eye(n):
    rows = lax.broadcasted_iota(jnp.int32, (n, n), 0)
    cols = lax.broadcasted_iota(jnp.int32, (n, n), 1)
    return jnp.where(rows == cols, 1.0, 0.0).astype(BF16)


def windows(ref, pieces, ps, flip):
    chan = ref.shape[-1]
    stacked = []
    for r0, r1, t0, t1 in pieces:
        taps = []
        for a in range(3):
            for b in range(3):
                da, db = (2 - a, 2 - b) if flip else (a, b)
                taps.append(
                    ref[r0 + da : r1 + da, (t0 + db) * ps : (t1 + db) * ps, :].reshape(
                        (r1 - r0) * (t1 - t0) * ps, chan
                    )
                )
        stacked.append(jnp.concatenate(taps, axis=1))
    return jnp.concatenate(stacked, axis=0) if len(stacked) > 1 else stacked[0]


def taps_nt(w_ref):
    return jnp.concatenate([w_ref[a, b] for a in range(3) for b in range(3)], axis=1)


def pieces_of(rows):
    inner = [(1, rows - 1, 1, POOL - 1)]
    outer = [
        (1, rows - 1, 0, 1),
        (1, rows - 1, POOL - 1, POOL),
        (0, 1, 0, POOL),
        (rows - 1, rows, 0, POOL),
    ]
    return inner, outer


def slabs_of(pieces):
    return [(r, t) for r0, r1, t0, t1 in pieces for r in range(r0, r1) for t in range(t0, t1)]


def make_kernel(lon_n, lat_n, rows, cols, chan, width):
    pr, ps = rows // POOL, cols // POOL
    keys = pr * ps
    heads = width // HEAD_DIM
    hq = heads * ps
    group = chan // HEAD_DIM
    groups = heads // group
    gq = group * ps
    slab_rows = (POOL + 2) * ps
    chips = lon_n // 2
    inner, outer = pieces_of(rows)
    half = ps // 2
    halo = [
        (0, 0, 1, 0), (1, 0, -1, 0),
        (0, 1, 1, 1), (1, 1, -1, 1),
        (0, 2, 1, -1), (1, 2, -1, -1),
    ]

    def kernel(
        field, conv_w, wq_h, wk_h, wv_h, qrow, ag_h,
        attended, cg, gin,
        xr, xs, cw, wq, wk, wv, ag,
        cout, dsl, nall, chosen, ntr, ex, dpr, pt, utb, gall, part, recv,
        stat, joined, colmsg, colhalo, dslrow, dslhalo, pgb, pgmid, pgcor, pgrow,
        load_sem, send_sem, recv_sem,
    ):
        lon = lax.axis_index("lon")
        lat = lax.axis_index("lat")
        count = itertools.count()

        def at(dlon, dlat):
            return {
                "lon": lax.rem(lon + dlon + lon_n, lon_n),
                "lat": lax.rem(lat + dlat + lat_n, lat_n),
            }

        sibling = {"lon": lon + 1 - 2 * lax.rem(lon, 2), "lat": lat}

        def remote(src, dst, device):
            k = next(count)
            return pltpu.make_async_remote_copy(
                src_ref=src,
                dst_ref=dst,
                send_sem=send_sem.at[k],
                recv_sem=recv_sem.at[k],
                device_id=device,
                device_id_type=MESH,
            )

        def start(copies):
            for c in copies:
                c.start()

        def wait(copies):
            for c in copies:
                c.wait()

        loads = [
            pltpu.make_async_copy(field, xr.at[pl.ds(1, rows)], load_sem.at[0]),
            pltpu.make_async_copy(conv_w, cw, load_sem.at[1]),
            pltpu.make_async_copy(ag_h.at[0], ag.at[0], load_sem.at[2]),
            pltpu.make_async_copy(wv_h, wv, load_sem.at[3]),
            pltpu.make_async_copy(wq_h, wq, load_sem.at[4]),
            pltpu.make_async_copy(wk_h, wk, load_sem.at[5]),
        ]
        loads[0].start()

        barrier = pltpu.get_barrier_semaphore()
        friends = [(0, -1), (0, 1)] + [(dlon, dlat) for _, _, dlon, dlat in halo]
        friends += [(2 * e, 0) for e in range(1, chips)]
        for dlon, dlat in friends:
            pl.semaphore_signal(barrier, inc=1, device_id=at(dlon, dlat), device_id_type=MESH)
        start(loads[1:])

        def columns(phase):
            return [
                remote(colmsg.at[phase, side], colhalo.at[phase, side, place], at(dlon, dlat))
                for side, place, dlon, dlat in halo
            ]

        loads[0].wait()
        for i in range(rows):
            colmsg[0, 0, i : i + 1, :] = xr[1 + i, cols - 16 : cols, :].astype(F32)[15:16]
            colmsg[0, 1, i : i + 1, :] = xr[1 + i, 0:16, :].astype(F32)[0:1]
        pl.semaphore_wait(barrier, len(friends))
        field_rows = [
            remote(field.at[0], xr.at[rows + 1], at(0, -1)),
            remote(field.at[rows - 1], xr.at[0], at(0, 1)),
        ]
        field_cols = columns(0)
        grads = remote(ag_h.at[0], ag.at[1], sibling)
        start(field_rows + field_cols + [grads])

        prow = lax.broadcasted_iota(jnp.int32, (slab_rows, cols), 0)
        pcol = lax.broadcasted_iota(jnp.int32, (slab_rows, cols), 1)
        spread = jnp.where(
            pcol == lax.rem(prow, ps) * POOL + lax.div(prow, ps) - 1, 1.0, 0.0
        ).astype(BF16)
        tile_row = lax.broadcasted_iota(jnp.int32, (16, chan), 0)

        def patch(ref, r, left, right):
            end = slab_rows - 16
            ref[r, 0:16, :] = jnp.where(tile_row == 0, left, ref[r, 0:16, :].astype(F32)).astype(
                BF16
            )
            ref[r, end:slab_rows, :] = jnp.where(
                tile_row == 15, right, ref[r, end:slab_rows, :].astype(F32)
            ).astype(BF16)

        for i in range(rows):
            xs[1 + i] = mm(spread, xr[1 + i]).astype(BF16)

        def convolve(pieces):
            y = mm(windows(xs, pieces, ps, False), cw[...].reshape(9 * chan, chan))
            for k, (r, t) in enumerate(slabs_of(pieces)):
                at_row = r * cols + t * ps
                cout[at_row : at_row + ps, :] = y[k * ps : (k + 1) * ps]

        loads[1].wait()
        convolve(inner)

        hrow = lax.div(lax.broadcasted_iota(jnp.int32, (gq, chan), 0), ps)
        hcol = lax.div(lax.broadcasted_iota(jnp.int32, (gq, chan), 1), HEAD_DIM)
        head_mask = hrow == hcol

        def absorb(x, w_ref, base, scale):
            for g in range(groups):
                x_g = x[:, g * chan : (g + 1) * chan]
                wide = jnp.where(head_mask, jnp.concatenate([x_g] * group, axis=0), 0.0)
                y = mm(wide.astype(BF16), w_ref[:, g * chan : (g + 1) * chan], NT)
                y = y * scale if scale != 1.0 else y
                gall[base + g * gq : base + (g + 1) * gq, :] = y.astype(BF16)

        loads[2].wait()
        loads[3].wait()
        absorb(ag[0].astype(F32), wv, 0, 1.0)

        wait(field_cols)
        for i in range(rows):
            patch(
                xs, 1 + i, colhalo[0, 0, 0, i : i + 1, :], colhalo[0, 1, 0, i : i + 1, :]
            )
        wait(field_rows)
        for r, place, pick, pole in ((0, 1, rows - 1, 0), (rows + 1, 2, 0, lat_n - 1)):
            xs[r] = mm(spread, xr[r]).astype(BF16)
            patch(
                xs,
                r,
                colhalo[0, 0, place, pick : pick + 1, :],
                colhalo[0, 1, place, pick : pick + 1, :],
            )
            xs[r] = jnp.where(lat == pole, 0.0, xs[r].astype(F32)).astype(BF16)
        convolve(outer)

        pooled = []
        for p in range(pr):
            v = cout[p * POOL * cols : (p + 1) * POOL * cols, :]
            act = v * (0.5 * jnp.tanh(0.5 * v) + 0.5)
            pooled.append(act.reshape(POOL * POOL, ps, chan).sum(axis=0) * (1.0 / (POOL * POOL)))
        pooled = jnp.concatenate(pooled, axis=0)
        centred = pooled - pooled.mean(-1, keepdims=True)
        inv_std = lax.rsqrt((centred * centred).mean(-1, keepdims=True) + NORM_EPS)
        standard = centred * inv_std
        nall[0] = standard.astype(BF16)
        first = qrow[0] == 0
        chosen[0] = jnp.where(first, standard[:ps], standard[ps:]).astype(BF16)

        order = [e for e in range(1, chips, 2)] + [e for e in range(2, chips, 2)]
        gathers = [remote(nall.at[0], nall.at[e], at(2 * e, 0)) for e in order]
        picks = remote(chosen.at[0], chosen.at[1], sibling)
        start([picks] + gathers)

        loads[4].wait()
        loads[5].wait()
        picks.wait()
        q = mm(chosen[...].reshape(2 * ps, chan), wq[...]).astype(BF16).astype(F32)
        absorb(q[:ps], wk, 2 * hq, HEAD_DIM**-0.5)
        absorb(q[ps:], wk, 3 * hq, HEAD_DIM**-0.5)
        grads.wait()
        absorb(ag[1].astype(F32), wv, hq, 1.0)
        for i in range(rows):
            v = cout[i * cols : (i + 1) * cols, :]
            sig = 0.5 * jnp.tanh(0.5 * v) + 0.5
            d = sig * (1.0 + v * (1.0 - sig)) * (1.0 / (POOL * POOL))
            dsl[i * cols : (i + 1) * cols, :] = d
            colmsg[1, 1, i : i + 1, :] = d[0:1]
            colmsg[1, 0, i : i + 1, :] = d[cols - 1 : cols]
            if i == 0:
                dslrow[0] = d.astype(BF16)
            if i == rows - 1:
                dslrow[1] = d.astype(BF16)
        ident = eye(chan)

        wait(gathers)
        slope_rows = [
            remote(dslrow.at[0], dslhalo.at[1], at(0, -1)),
            remote(dslrow.at[1], dslhalo.at[0], at(0, 1)),
        ]
        slope_cols = columns(1)
        start(slope_rows + slope_cols)

        nv = nall[...].reshape(chips * keys, chan)
        blk = chan
        for h0 in range(0, 2 * hq, blk):
            s = mm(nv, gall[2 * hq + h0 : 2 * hq + h0 + blk, :], NT)
            top = s.max(axis=0, keepdims=True)
            e = jnp.exp(s - top)
            dp = mm(nv, gall[h0 : h0 + blk, :], NT)
            ex[:, h0 : h0 + blk] = e
            dpr[:, h0 : h0 + blk] = dp
            stat[0, 0:1, h0 : h0 + blk] = top
            stat[0, 1:2, h0 : h0 + blk] = e.sum(axis=0, keepdims=True)
            stat[0, 2:3, h0 : h0 + blk] = (e * dp).sum(axis=0, keepdims=True)
        stats = remote(stat.at[0], stat.at[1], sibling)
        stats.start()
        ntr[...] = mm(ident, nv, NT).astype(BF16)
        stats.wait()
        for h0 in range(0, 2 * hq, blk):
            o0 = (h0 + hq) % (2 * hq)
            top, size, dot = (stat[0, k : k + 1, h0 : h0 + blk] for k in range(3))
            top2, size2, dot2 = (stat[1, k : k + 1, o0 : o0 + blk] for k in range(3))
            peak = jnp.maximum(top, top2)
            f, f2 = jnp.exp(top - peak), jnp.exp(top2 - peak)
            inv = 1.0 / (size * f + size2 * f2)
            delta = (dot * f + dot2 * f2) * inv
            prob = ex[:, h0 : h0 + blk] * (f * inv)
            pt[:, h0 : h0 + blk] = prob.astype(BF16)
            pt[:, 2 * hq + h0 : 2 * hq + h0 + blk] = (
                prob * (dpr[:, h0 : h0 + blk] - delta)
            ).astype(BF16)

        scatters = {}
        own = None
        step = chips // 2
        for d0 in (step, 0):
            y = mm(pt[d0 * keys : (d0 + step) * keys, :], gall[...])
            if d0 == 0:
                own = y[:keys]
            part[d0 : d0 + step] = y.astype(BF16).reshape(step, keys, chan)
            for e in range(max(d0, 1), d0 + step):
                scatters[e] = remote(part.at[e], recv.at[e], at(-2 * e, 0))
                scatters[e].start()

        utb[...] = mm(ntr[...], pt[...]).astype(BF16)
        ident_g = eye(gq)
        mine = None
        for owner in (1, 0):
            outs = []
            qfeat = jnp.zeros((ps, chan), F32)
            for g in range(groups):
                for which in range(2):
                    c0 = (2 * which + owner) * hq + g * gq
                    u = mm(ident_g, utb[:, c0 : c0 + gq], NT).astype(BF16)
                    w = (wv, wk)[which][:, g * chan : (g + 1) * chan]
                    y = jnp.where(head_mask, mm(u, w), 0.0).reshape(group, ps, chan).sum(axis=0)
                    if which == 0:
                        outs.append(y)
                    else:
                        y = (y * HEAD_DIM**-0.5).astype(BF16)
                        qfeat = qfeat + mm(y, wq[:, g * chan : (g + 1) * chan], NT)
            if owner == 1:
                for g in range(groups):
                    joined[0, :, g * chan : (g + 1) * chan] = outs[g]
                joined[0, :, width : width + chan] = qfeat
                joins = remote(joined.at[0], joined.at[1], sibling)
                joins.start()
            else:
                mine = (outs, qfeat)
        joins.wait()
        outs, qfeat = mine
        for g in range(groups):
            cell = slice(g * chan, (g + 1) * chan)
            attended[0, :, cell] = (outs[g] + joined[1, :, cell]).astype(BF16)
        qfeat = qfeat + joined[1, :, width : width + chan]

        zero = jnp.zeros_like(qfeat)
        total = own + jnp.concatenate(
            [jnp.where(first, qfeat, zero), jnp.where(first, zero, qfeat)], axis=0
        )
        wait(slope_rows + slope_cols)
        wait(scatters.values())
        total = total + recv[1:].astype(F32).sum(axis=0)
        pgrad = inv_std * (
            total
            - total.mean(-1, keepdims=True)
            - standard * (total * standard).mean(-1, keepdims=True)
        )
        pgb[...] = pgrad.astype(BF16).reshape(pr, ps, chan)
        sides = (pl.ds(ps - half, half), pl.ds(0, half))
        pg_rows = [
            remote(pgb.at[0], pgrow.at[1], at(0, -1)),
            remote(pgb.at[pr - 1], pgrow.at[0], at(0, 1)),
        ]
        pg_cols = []
        for side, place, dlon, dlat in halo:
            if place == 0:
                src, dst = pgb.at[:, sides[side]], pgmid.at[side]
            else:
                src = pgb.at[pr - 1 if place == 1 else 0, sides[side]]
                dst = pgcor.at[side, place - 1]
            pg_cols.append(remote(src, dst, at(dlon, dlat)))
        start(pg_rows + pg_cols)

        def grad_row(r, pg, slope):
            slabs = [pg * slope[t * ps : (t + 1) * ps] for t in range(POOL)]
            cg[r, 0:ps, :] = pltpu.roll(slabs[POOL - 1], 1, 0).astype(BF16)
            cg[r, slab_rows - ps : slab_rows, :] = pltpu.roll(slabs[0], ps - 1, 0).astype(BF16)
            for t in range(POOL):
                cg[r, (t + 1) * ps : (t + 2) * ps, :] = slabs[t].astype(BF16)

        for i in range(rows):
            p = i // POOL
            grad_row(1 + i, pgrad[p * ps : (p + 1) * ps], dsl[i * cols : (i + 1) * cols, :])
        gin[...] = mm(windows(cg, inner, ps, True), taps_nt(cw), NT).astype(BF16)

        wait(pg_cols)
        lefts = [pgmid[0, p].astype(F32)[half - 1 : half] for p in range(pr)]
        rights = [pgmid[1, p].astype(F32)[0:1] for p in range(pr)]
        for i in range(rows):
            patch(
                cg,
                1 + i,
                lefts[i // POOL] * colhalo[1, 0, 0, i : i + 1, :],
                rights[i // POOL] * colhalo[1, 1, 0, i : i + 1, :],
            )
        wait(pg_rows)
        for r, place, pick, pole in ((0, 1, rows - 1, 0), (rows + 1, 2, 0, lat_n - 1)):
            there = jnp.where(lat == pole, 0.0, 1.0)
            grad_row(r, pgrow[place - 1].astype(F32) * there, dslhalo[place - 1].astype(F32))
            patch(
                cg,
                r,
                pgcor[0, place - 1].astype(F32)[half - 1 : half]
                * colhalo[1, 0, place, pick : pick + 1, :]
                * there,
                pgcor[1, place - 1].astype(F32)[0:1]
                * colhalo[1, 1, place, pick : pick + 1, :]
                * there,
            )

    return kernel


def make_final(rows, cols, chan):
    ps = cols // POOL
    inner, outer = pieces_of(rows)

    def kernel(cg, gin, cw, att, attended, out_grad, slab, obuf, sem):
        send_att = pltpu.make_async_copy(att, attended, sem.at[rows])
        send_att.start()
        y = mm(windows(cg, outer, ps, True), taps_nt(cw), NT).astype(BF16)
        where = {}
        for k, rt in enumerate(slabs_of(outer)):
            where[rt] = y[k * ps : (k + 1) * ps]
        for k, rt in enumerate(slabs_of(inner)):
            where[rt] = gin[k * ps : (k + 1) * ps, :]
        prow = lax.broadcasted_iota(jnp.int32, (cols, cols), 0)
        pcol = lax.broadcasted_iota(jnp.int32, (cols, cols), 1)
        weave = jnp.where(
            prow == lax.rem(pcol, ps) * POOL + lax.div(pcol, ps), 1.0, 0.0
        ).astype(BF16)
        stores = [send_att]
        for i in range(rows):
            line = jnp.concatenate([where[i, t] for t in range(POOL)], axis=0)
            obuf[i] = mm(weave, line).astype(BF16)
            store = pltpu.make_async_copy(obuf.at[i], out_grad.at[i], sem.at[i])
            store.start()
            stores.append(store)
        for store in stores:
            store.wait()

    return kernel


def solution(mesh):
    lon_n, lat_n = mesh.shape["lon"], mesh.shape["lat"]

    def on_device(field, conv_w, wq, wk, wv, query_rows, attended_grad):
        rows, cols, chan = field.shape
        width = wq.shape[1]
        pr, ps = rows // POOL, cols // POOL
        keys = pr * ps
        chips = lon_n // 2
        hq = (width // HEAD_DIM) * ps
        slab_rows = (POOL + 2) * ps
        gin_rows = (rows - 2) * (POOL - 2) * ps
        any_spec = pl.BlockSpec(memory_space=pl.ANY)
        vmem = pl.BlockSpec(memory_space=pltpu.VMEM)
        att, cg, gin = pl.pallas_call(
            make_kernel(lon_n, lat_n, rows, cols, chan, width),
            out_shape=(
                pltpu.VMEM(attended_grad.shape, BF16),
                pltpu.VMEM((rows + 2, slab_rows, chan), BF16),
                pltpu.VMEM((gin_rows, chan), BF16),
            ),
            in_specs=[any_spec] * 5 + [vmem, any_spec],
            out_specs=(vmem, vmem, vmem),
            scratch_shapes=[
                pltpu.VMEM((rows + 2, cols, chan), BF16),
                pltpu.VMEM((rows + 2, slab_rows, chan), BF16),
                pltpu.VMEM((3, 3, chan, chan), BF16),
                pltpu.VMEM((chan, width), BF16),
                pltpu.VMEM((chan, width), BF16),
                pltpu.VMEM((chan, width), BF16),
                pltpu.VMEM((2, ps, width), BF16),
                pltpu.VMEM((rows * cols, chan), F32),
                pltpu.VMEM((rows * cols, chan), F32),
                pltpu.VMEM((chips, keys, chan), BF16),
                pltpu.VMEM((2, ps, chan), BF16),
                pltpu.VMEM((chan, chips * keys), BF16),
                pltpu.VMEM((chips * keys, 2 * hq), F32),
                pltpu.VMEM((chips * keys, 2 * hq), F32),
                pltpu.VMEM((chips * keys, 4 * hq), BF16),
                pltpu.VMEM((chan, 4 * hq), BF16),
                pltpu.VMEM((4 * hq, chan), BF16),
                pltpu.VMEM((chips, keys, chan), BF16),
                pltpu.VMEM((chips, keys, chan), BF16),
                pltpu.VMEM((2, 8, 2 * hq), F32),
                pltpu.VMEM((2, ps, width + chan), F32),
                pltpu.VMEM((2, 2, rows, chan), F32),
                pltpu.VMEM((2, 2, 3, rows, chan), F32),
                pltpu.VMEM((2, cols, chan), BF16),
                pltpu.VMEM((2, cols, chan), BF16),
                pltpu.VMEM((pr, ps, chan), BF16),
                pltpu.VMEM((2, pr, ps // 2, chan), BF16),
                pltpu.VMEM((2, 2, ps // 2, chan), BF16),
                pltpu.VMEM((2, ps, chan), BF16),
                pltpu.SemaphoreType.DMA((6,)),
                pltpu.SemaphoreType.DMA((48,)),
                pltpu.SemaphoreType.DMA((48,)),
            ],
            compiler_params=pltpu.CompilerParams(
                collective_id=0, has_side_effects=True, vmem_limit_bytes=55 * 1024 * 1024
            ),
        )(field, conv_w, wq, wk, wv, query_rows, attended_grad)
        return pl.pallas_call(
            make_final(rows, cols, chan),
            out_shape=(
                jax.ShapeDtypeStruct(attended_grad.shape, BF16),
                jax.ShapeDtypeStruct(field.shape, BF16),
            ),
            in_specs=[vmem] * 4,
            out_specs=(any_spec, any_spec),
            scratch_shapes=[
                pltpu.VMEM((POOL * ps, chan), BF16),
                pltpu.VMEM((rows, cols, chan), BF16),
                pltpu.SemaphoreType.DMA((rows + 1,)),
            ],
            compiler_params=pltpu.CompilerParams(vmem_limit_bytes=20 * 1024 * 1024),
        )(cg, gin, conv_w, att)

    return jax.shard_map(
        on_device,
        mesh=mesh,
        in_specs=(
            P("lat", "lon", None),
            P(),
            P(),
            P(),
            P(),
            P("lat", "lon", None),
            P("lat", "lon", None),
        ),
        out_specs=(P("lat", "lon", None), P("lat", "lon", None)),
        check_vma=False,
    )
```

time: 258 us -> 46.9 us (0.18)
  waiting for transfers between devices: 151 us -> 0 us
  Pallas kernels: 0 us -> 45.5 us
  starting transfers between devices: 39.6 us -> 0 us
  matrix products: 26 us -> 0 us
  local copies, waits for them, and re-layouts: 16.5 us -> 0.01 us
  between operations: 14.9 us -> 1.3 us
  other arithmetic: 9.01 us -> 0 us
    all_gather x2 -> x0, waiting for transfers between devices: 71.8 us -> none  [the longest x1 38 us: on_device(): lax.all_gather(value_rows, 'lon', axis=0, tiled=True)]
    reduce_scatter x1 -> x0, waiting for transfers between devices: 63.3 us -> none  [on_device(): lax.psum_scatter((feat_term + jnp.einsum('ka,ca->kc', value_part.reshape(...]
    pallas_call x0 -> x2, Pallas kernels: none -> 45.5 us  [the longest x1 43.4 us: on_device(): pl.pallas_call(make_kernel(lon_n, lat_n, rows, cols, chan, width), out_sh...]
    ppermute x8 -> x0, starting transfers between devices: 39.3 us -> none  [the longest x4 31.7 us: with_halo(): lax.ppermute(head, axis, [((i + 1) % count, i) for i in range(count)])]
    dot_general x31 -> x0, matrix products: 26 us -> none  [the longest x18 6.43 us: convolve(): jnp.dot(window, kernel[tap_row, tap_col], preferred_element_type=jnp.floa...]
    ppermute x8 -> x0, waiting for transfers between devices: 15.7 us -> none  [the longest x4 15.7 us: with_halo(): lax.ppermute(tail, axis, [(i, (i + 1) % count) for i in range(count)])]
    all_gather x2 -> x0, local copies, waits for them, and re-layouts: 6.78 us -> none  [the longest x1 3.92 us: on_device(): lax.all_gather(value_rows, 'lon', axis=0, tiled=True)]
    reshape x6 -> x0, local copies, waits for them, and re-layouts: 3.1 us -> none  [the longest x1 1.58 us: on_device(): spread_grad = jnp.broadcast_to((pooled_grad / 16.0)[:, None, :, None, :],...]
  transfers between devices with their start and end apart: 11 -> 0, of which waited for: 7 -> 0; matrix products, arithmetic and copies ran while one was open for 4% -> 0% of each run, Pallas kernels for 0% -> 0%
where the time goes in v2:
time: 46.9 us; the launch traced here: 46.8 us
  Pallas kernels  45.5 us (97%)
  between operations  1.3 us (3%)
    pallas_call x1, Pallas kernels, on_device(): pl.pallas_call(make_kernel(lon_n, lat_n, rows, cols, chan, width), out_sh...  43.4 us
    pallas_call x1, Pallas kernels, on_device(): pl.pallas_call(make_final(rows, cols, chan), out_shape=(jax.ShapeDtypeStr...  2.14 us

profile of v2, /device:TPU:1, one launch (start us, length us, event | category | flops | bytes accessed | tf_op | source)
XLA Modules:
  0.0 46.8 jit_solution(3233334226022866981)
XLA Ops:
  1.3 0.0 copy-start
  1.3 43.4 %shard_map.86 = (bf16[1,32,1024]{2,1,0:T(8,128)(2,1)S(1)}, bf16[10,192,256]{2,1,0:T(8,128)(2,1)S(1)}, bf16[384,256]{1,0:T(8,128)(2,1)S(1)}) custom-call(bf16[8,128,256]{2,1,0:T(8,128)(2,1)} %field.1, bf16[3,3,256,256]{3,2,1,0:T(8,128)(2,1)} %cw.1, bf16[256,1024]{1,0:T(8,128)(2,1)} %wq_h.1, bf16[256,1024]{1,0:T(8,128)(2,1)} %wk_h.1, bf16[256,1024]{1,0:T(8,128)(2,1)} %wv_h.1, ...), custom_call_target="tpu_custom_call" | custom-call | tf_op jit(solution)/shard_map/pallas_call | solution.py:455
  44.7 0.0 copy-done
  44.7 2.1 %shard_map.87 = (bf16[1,32,1024]{2,1,0:T(8,128)(2,1)}, bf16[8,128,256]{2,1,0:T(8,128)(2,1)}) custom-call(bf16[10,192,256]{2,1,0:T(8,128)(2,1)S(1)} %get-tuple-element.5.cg, bf16[384,256]{1,0:T(8,128)(2,1)S(1)} %get-tuple-element.6.gin, bf16[3,3,256,256]{3,2,1,0:T(8,128)(2,1)S(1)} %copy-done, bf16[1,32,1024]{2,1,0:T(8,128)(2,1)S(1)} %get-tuple-element.7.att), custom_call_target="tpu_custom_call" | custom-call | tf_op jit(solution)/shard_map/pallas_call | solution.py:502
Async XLA Ops:
  1.3 43.4 %copy-start = (bf16[3,3,256,256]{3,2,1,0:T(8,128)(2,1)S(1)}, bf16[3,3,256,256]{3,2,1,0:T(8,128)(2,1)}, u32[]{:S(2)}) copy-start(bf16[3,3,256,256]{3,2,1,0:T(8,128)(2,1)} %cw.1) | copy-start | bytes 3538948

commit v3 on v2

v3 whole, which is shorter than its diff:
```python
import itertools

import jax
import jax.numpy as jnp
from jax import lax
from jax.experimental import pallas as pl
from jax.experimental.pallas import tpu as pltpu
from jax.sharding import PartitionSpec as P

HEAD_DIM = 64
NORM_EPS = 1e-05
POOL = 4
BF16 = jnp.bfloat16
F32 = jnp.float32
MESH = pl.DeviceIdType.MESH

NN = (((1,), (0,)), ((), ()))
NT = (((1,), (1,)), ((), ()))


def mm(a, b, dims=NN):
    return lax.dot_general(a, b, dims, preferred_element_type=F32)


def eye(n):
    rows = lax.broadcasted_iota(jnp.int32, (n, n), 0)
    cols = lax.broadcasted_iota(jnp.int32, (n, n), 1)
    return jnp.where(rows == cols, 1.0, 0.0).astype(BF16)


def windows(ref, rows, cols, ps, flip):
    chan = ref.shape[-1]
    taps = []
    for a in range(3):
        for b in range(3):
            da, db = (2 - a, 2 - b) if flip else (a, b)
            taps.append(
                ref[da : da + rows, db * ps : db * ps + cols, :].reshape(rows * cols, chan)
            )
    return jnp.concatenate(taps, axis=1)


def silu(v):
    return v * (0.5 * jnp.tanh(0.5 * v) + 0.5)


def make_kernel(lon_n, lat_n, rows, cols, chan, width):
    pr, ps = rows // POOL, cols // POOL
    keys = pr * ps
    heads = width // HEAD_DIM
    hq = heads * ps
    group = chan // HEAD_DIM
    groups = heads // group
    gq = group * ps
    slab_rows = (POOL + 2) * ps
    chips = lon_n // 2
    half = ps // 2
    slot_shift = list(range(0, chips, 2)) + list(range(1, chips, 2))
    split = chips // 2
    halo = [
        (0, 0, 1, 0), (1, 0, -1, 0),
        (0, 1, 1, 1), (1, 1, -1, 1),
        (0, 2, 1, -1), (1, 2, -1, -1),
    ]

    def kernel(
        field, conv_w, wq_h, wk_h, wv_h, qrow, ag_h,
        attended, gout,
        xr, xs, xh, cg, ch, cw, wq, wk, wv, ag,
        cout, ccol, grow, dsl, nall, chosen, ntr, ex, dpr, pt, utb, gall, part, recv,
        stat, joined, colmsg, colhalo, dslrow, dslhalo, pgb, pgmid, pgcor, pgrow,
        load_sem, send_sem, recv_sem,
    ):
        lon = lax.axis_index("lon")
        lat = lax.axis_index("lat")
        count = itertools.count()

        def at(dlon, dlat):
            return {
                "lon": lax.rem(lon + dlon + lon_n, lon_n),
                "lat": lax.rem(lat + dlat + lat_n, lat_n),
            }

        sibling = {"lon": lon + 1 - 2 * lax.rem(lon, 2), "lat": lat}

        def remote(src, dst, device):
            k = next(count)
            return pltpu.make_async_remote_copy(
                src_ref=src,
                dst_ref=dst,
                send_sem=send_sem.at[k],
                recv_sem=recv_sem.at[k],
                device_id=device,
                device_id_type=MESH,
            )

        def start(copies):
            for c in copies:
                c.start()

        def wait(copies):
            for c in copies:
                c.wait()

        loads = [
            pltpu.make_async_copy(field, xr, load_sem.at[0]),
            pltpu.make_async_copy(conv_w, cw, load_sem.at[1]),
            pltpu.make_async_copy(ag_h.at[0], ag.at[0], load_sem.at[2]),
            pltpu.make_async_copy(wv_h, wv, load_sem.at[3]),
            pltpu.make_async_copy(wq_h, wq, load_sem.at[4]),
            pltpu.make_async_copy(wk_h, wk, load_sem.at[5]),
        ]
        loads[0].start()

        barrier = pltpu.get_barrier_semaphore()
        friends = [(0, -1), (0, 1)] + [(dlon, dlat) for _, _, dlon, dlat in halo]
        friends += [(2 * e, 0) for e in range(1, chips)]
        for dlon, dlat in friends:
            pl.semaphore_signal(barrier, inc=1, device_id=at(dlon, dlat), device_id_type=MESH)
        start(loads[1:])

        def columns(phase):
            return [
                remote(colmsg.at[phase, side], colhalo.at[phase, side, place], at(dlon, dlat))
                for side, place, dlon, dlat in halo
            ]

        prow = lax.broadcasted_iota(jnp.int32, (slab_rows, cols), 0)
        pcol = lax.broadcasted_iota(jnp.int32, (slab_rows, cols), 1)
        spread = jnp.where(
            pcol == lax.rem(prow, ps) * POOL + lax.div(prow, ps) - 1, 1.0, 0.0
        ).astype(BF16)
        mid = pl.ds(ps, cols)

        loads[0].wait()
        for i in (0, rows - 1):
            xs[1 + i] = mm(spread, xr[i]).astype(BF16)
        for i in range(rows):
            colmsg[0, 0, i : i + 1, :] = xr[i, cols - 16 : cols, :].astype(F32)[15:16]
            colmsg[0, 1, i : i + 1, :] = xr[i, 0:16, :].astype(F32)[0:1]
        pl.semaphore_wait(barrier, len(friends))
        field_rows = [
            remote(xs.at[1, mid], xh.at[1, mid], at(0, -1)),
            remote(xs.at[rows, mid], xh.at[0, mid], at(0, 1)),
        ]
        field_cols = columns(0)
        grads = remote(ag_h.at[0], ag.at[1], sibling)
        start(field_rows + field_cols + [grads])

        xs[0] = jnp.zeros((slab_rows, chan), BF16)
        xs[rows + 1] = jnp.zeros((slab_rows, chan), BF16)
        for i in range(1, rows - 1):
            xs[1 + i] = mm(spread, xr[i]).astype(BF16)
        loads[1].wait()
        cout[...] = mm(windows(xs, rows, cols, ps, False), cw[...].reshape(9 * chan, chan))
        pooled = []
        for p in range(pr):
            lo, hi = max(p * POOL, 1), min((p + 1) * POOL, rows - 1)
            act = silu(cout[lo * cols : hi * cols, :])
            pooled.append(act.reshape((hi - lo) * POOL, ps, chan).sum(axis=0))
        for i in range(rows):
            ccol[0, i : i + 1, :] = cout[i * cols : i * cols + 1, :]
            ccol[1, i : i + 1, :] = cout[(i + 1) * cols - 1 : (i + 1) * cols, :]

        edge = lax.broadcasted_iota(jnp.int32, (ps, chan), 0)
        line = lax.broadcasted_iota(jnp.int32, (rows, chan), 0)

        def column_taps(cells):
            above = jnp.where(line == 0, 0.0, pltpu.roll(cells, 1, 0))
            below = jnp.where(line == rows - 1, 0.0, pltpu.roll(cells, rows - 1, 0))
            return above, cells, below

        def column_terms(left, right, weights, dims):
            none = jnp.zeros((rows, 3 * chan), F32)
            left, right = jnp.concatenate(left, axis=1), jnp.concatenate(right, axis=1)
            lhs = jnp.concatenate(
                [
                    jnp.concatenate([left, none], axis=1),
                    jnp.concatenate([none, right], axis=1),
                ],
                axis=0,
            ).astype(BF16)
            axis = 1 if dims == NT else 0
            y = mm(lhs, jnp.concatenate(weights, axis=axis), dims)
            return y[:rows], y[rows:]

        def row_slabs(ref, k, first_slab, last_slab, left, right):
            lo = pltpu.roll(last_slab, 1, 0)
            hi = pltpu.roll(first_slab, ps - 1, 0)
            ref[k, 0:ps, :] = jnp.where(edge == 0, left, lo).astype(BF16)
            ref[k, slab_rows - ps : slab_rows, :] = jnp.where(edge == ps - 1, right, hi).astype(
                BF16
            )

        hrow = lax.div(lax.broadcasted_iota(jnp.int32, (gq, chan), 0), ps)
        hcol = lax.div(lax.broadcasted_iota(jnp.int32, (gq, chan), 1), HEAD_DIM)
        head_mask = hrow == hcol

        def absorb(x, w_ref, base, scale):
            for g in range(groups):
                x_g = x[:, g * chan : (g + 1) * chan]
                wide = jnp.where(head_mask, jnp.concatenate([x_g] * group, axis=0), 0.0)
                y = mm(wide.astype(BF16), w_ref[:, g * chan : (g + 1) * chan], NT)
                y = y * scale if scale != 1.0 else y
                gall[base + g * gq : base + (g + 1) * gq, :] = y.astype(BF16)

        loads[2].wait()
        loads[3].wait()
        absorb(ag[0].astype(F32), wv, 0, 1.0)

        wait(field_cols)
        fixes = column_terms(
            column_taps(colhalo[0, 0, 0]),
            column_taps(colhalo[0, 1, 0]),
            [cw[a, 0] for a in range(3)] + [cw[a, 2] for a in range(3)],
            NN,
        )
        for side in range(2):
            before = ccol[side]
            after = before + fixes[side]
            ccol[side] = after
            change = silu(after) - silu(before)
            cell = edge == (0, ps - 1)[side]
            for p in range(pr):
                lo, hi = max(p * POOL, 1), min((p + 1) * POOL, rows - 1)
                part_sum = jnp.where((line >= lo) & (line < hi), change, 0.0).sum(
                    axis=0, keepdims=True
                )
                pooled[p] = pooled[p] + jnp.where(cell, part_sum, 0.0)
        for i in range(rows):
            cout[i * cols : i * cols + 1, :] = ccol[0, i : i + 1, :]
            cout[(i + 1) * cols - 1 : (i + 1) * cols, :] = ccol[1, i : i + 1, :]
        wait(field_rows)
        for k, pick, pole in ((0, rows - 1, 0), (1, 0, lat_n - 1)):
            there = jnp.where(lat == pole, 0.0, 1.0)
            row_slabs(
                xh,
                k,
                xh[k, ps : 2 * ps, :].astype(F32),
                xh[k, POOL * ps : (POOL + 1) * ps, :].astype(F32),
                colhalo[0, 0, 1 + k, pick : pick + 1, :],
                colhalo[0, 1, 1 + k, pick : pick + 1, :],
            )
            lhs = jnp.concatenate([xh[k, b * ps : b * ps + cols, :] for b in range(3)], axis=1)
            fix = mm(lhs, cw[2 * k].reshape(3 * chan, chan)) * there
            i = k * (rows - 1)
            v = cout[i * cols : (i + 1) * cols, :] + fix
            cout[i * cols : (i + 1) * cols, :] = v
            p = k * (pr - 1)
            pooled[p] = pooled[p] + silu(v).reshape(POOL, ps, chan).sum(axis=0)
        pooled = jnp.concatenate(pooled, axis=0) * (1.0 / (POOL * POOL))
        centred = pooled - pooled.mean(-1, keepdims=True)
        inv_std = lax.rsqrt((centred * centred).mean(-1, keepdims=True) + NORM_EPS)
        standard = centred * inv_std
        nall[0] = standard.astype(BF16)
        first = qrow[0] == 0
        chosen[0] = jnp.where(first, standard[:ps], standard[ps:]).astype(BF16)

        gathers = [
            remote(nall.at[0], nall.at[k], at(2 * slot_shift[k], 0)) for k in range(1, chips)
        ]
        picks = remote(chosen.at[0], chosen.at[1], sibling)
        start([picks] + gathers[split - 1 :] + gathers[: split - 1])

        loads[4].wait()
        loads[5].wait()
        picks.wait()
        q = mm(chosen[...].reshape(2 * ps, chan), wq[...]).astype(BF16).astype(F32)
        absorb(q[:ps], wk, 2 * hq, HEAD_DIM**-0.5)
        absorb(q[ps:], wk, 3 * hq, HEAD_DIM**-0.5)
        grads.wait()
        absorb(ag[1].astype(F32), wv, hq, 1.0)
        for i in range(rows):
            v = cout[i * cols : (i + 1) * cols, :]
            sig = 0.5 * jnp.tanh(0.5 * v) + 0.5
            d = sig * (1.0 + v * (1.0 - sig)) * (1.0 / (POOL * POOL))
            dsl[i * cols : (i + 1) * cols, :] = d
            colmsg[1, 1, i : i + 1, :] = d[0:1]
            colmsg[1, 0, i : i + 1, :] = d[cols - 1 : cols]
            if i == 0:
                dslrow[0] = d.astype(BF16)
            if i == rows - 1:
                dslrow[1] = d.astype(BF16)
        ident = eye(chan)

        blk = chan
        half_keys = split * keys

        def score(part_at):
            r0 = part_at * half_keys
            nv = nall[part_at * split : (part_at + 1) * split].reshape(half_keys, chan)
            for h0 in range(0, 2 * hq, blk):
                s = mm(nv, gall[2 * hq + h0 : 2 * hq + h0 + blk, :], NT)
                top = s.max(axis=0, keepdims=True)
                e = jnp.exp(s - top)
                dp = mm(nv, gall[h0 : h0 + blk, :], NT)
                ex[r0 : r0 + half_keys, h0 : h0 + blk] = e
                dpr[r0 : r0 + half_keys, h0 : h0 + blk] = dp
                k = 3 * part_at
                stat[0, k : k + 1, h0 : h0 + blk] = top
                stat[0, k + 1 : k + 2, h0 : h0 + blk] = e.sum(axis=0, keepdims=True)
                stat[0, k + 2 : k + 3, h0 : h0 + blk] = (e * dp).sum(axis=0, keepdims=True)
            return nv

        wait(gathers[: split - 1])
        score(0)
        wait(gathers[split - 1 :])
        score(1)
        stats = remote(stat.at[0], stat.at[1], sibling)
        stats.start()
        slope_rows = [
            remote(dslrow.at[0], dslhalo.at[1], at(0, -1)),
            remote(dslrow.at[1], dslhalo.at[0], at(0, 1)),
        ]
        slope_cols = columns(1)
        start(slope_rows + slope_cols)
        ntr[...] = mm(ident, nall[...].reshape(chips * keys, chan), NT).astype(BF16)
        stats.wait()
        scale = {}
        for h0 in range(0, 2 * hq, blk):
            o0 = (h0 + hq) % (2 * hq)
            tops, sizes, dots = (
                [
                    stat[who, 3 * q + k : 3 * q + k + 1, c0 : c0 + blk]
                    for who, c0 in ((0, h0), (1, o0))
                    for q in range(2)
                ]
                for k in range(3)
            )
            peak = jnp.maximum(jnp.maximum(tops[0], tops[1]), jnp.maximum(tops[2], tops[3]))
            f = [jnp.exp(t - peak) for t in tops]
            inv = 1.0 / sum(a * b for a, b in zip(sizes, f))
            delta = sum(a * b for a, b in zip(dots, f)) * inv
            scale[h0] = (f[0] * inv, f[1] * inv, delta)

        scatters = []
        own = None
        for part_at in (1, 0):
            r0 = part_at * half_keys
            for h0 in range(0, 2 * hq, blk):
                prob = ex[r0 : r0 + half_keys, h0 : h0 + blk] * scale[h0][part_at]
                pt[r0 : r0 + half_keys, h0 : h0 + blk] = prob.astype(BF16)
                pt[r0 : r0 + half_keys, 2 * hq + h0 : 2 * hq + h0 + blk] = (
                    prob * (dpr[r0 : r0 + half_keys, h0 : h0 + blk] - scale[h0][2])
                ).astype(BF16)
            y = mm(pt[r0 : r0 + half_keys, :], gall[...])
            if part_at == 0:
                own = y[:keys]
            part[part_at * split : (part_at + 1) * split] = y.astype(BF16).reshape(
                split, keys, chan
            )
            for k in range(max(part_at * split, 1), (part_at + 1) * split):
                scatters.append(remote(part.at[k], recv.at[k], at(-2 * slot_shift[k], 0)))
                scatters[-1].start()

        utb[...] = mm(ntr[...], pt[...]).astype(BF16)
        ident_g = eye(gq)
        mine = None
        for owner in (1, 0):
            outs = []
            qfeat = jnp.zeros((ps, chan), F32)
            for g in range(groups):
                for which in range(2):
                    c0 = (2 * which + owner) * hq + g * gq
                    u = mm(ident_g, utb[:, c0 : c0 + gq], NT).astype(BF16)
                    w = (wv, wk)[which][:, g * chan : (g + 1) * chan]
                    y = jnp.where(head_mask, mm(u, w), 0.0).reshape(group, ps, chan).sum(axis=0)
                    if which == 0:
                        outs.append(y)
                    else:
                        y = (y * HEAD_DIM**-0.5).astype(BF16)
                        qfeat = qfeat + mm(y, wq[:, g * chan : (g + 1) * chan], NT)
            if owner == 1:
                for g in range(groups):
                    joined[0, :, g * chan : (g + 1) * chan] = outs[g]
                joined[0, :, width : width + chan] = qfeat
                joins = remote(joined.at[0], joined.at[1], sibling)
                joins.start()
            else:
                mine = (outs, qfeat)
        joins.wait()
        outs, qfeat = mine
        for g in range(groups):
            cell = slice(g * chan, (g + 1) * chan)
            attended[0, :, cell] = (outs[g] + joined[1, :, cell]).astype(BF16)
        qfeat = qfeat + joined[1, :, width : width + chan]

        zero = jnp.zeros_like(qfeat)
        total = own + jnp.concatenate(
            [jnp.where(first, qfeat, zero), jnp.where(first, zero, qfeat)], axis=0
        )
        wait(slope_rows + slope_cols)
        wait(scatters)
        total = total + recv[1:].astype(F32).sum(axis=0)
        pgrad = inv_std * (
            total
            - total.mean(-1, keepdims=True)
            - standard * (total * standard).mean(-1, keepdims=True)
        )
        pgb[...] = pgrad.astype(BF16).reshape(pr, ps, chan)
        sides = (pl.ds(ps - half, half), pl.ds(0, half))
        pg_rows = [
            remote(pgb.at[0], pgrow.at[1], at(0, -1)),
            remote(pgb.at[pr - 1], pgrow.at[0], at(0, 1)),
        ]
        pg_cols = []
        for side, place, dlon, dlat in halo:
            if place == 0:
                src, dst = pgb.at[:, sides[side]], pgmid.at[side]
            else:
                src = pgb.at[pr - 1 if place == 1 else 0, sides[side]]
                dst = pgcor.at[side, place - 1]
            pg_cols.append(remote(src, dst, at(dlon, dlat)))
        start(pg_rows + pg_cols)

        cg[0] = jnp.zeros((slab_rows, chan), BF16)
        cg[rows + 1] = jnp.zeros((slab_rows, chan), BF16)
        for i in range(rows):
            p = i // POOL
            pg = pgrad[p * ps : (p + 1) * ps]
            slabs = [
                pg * dsl[i * cols + t * ps : i * cols + (t + 1) * ps, :] for t in range(POOL)
            ]
            for t in range(POOL):
                cg[1 + i, (t + 1) * ps : (t + 2) * ps, :] = slabs[t].astype(BF16)
            row_slabs(cg, 1 + i, slabs[0], slabs[POOL - 1], 0.0, 0.0)
        weights = jnp.concatenate([cw[a, b] for a in range(3) for b in range(3)], axis=1)
        y = mm(windows(cg, rows, cols, ps, True), weights, NT)
        wrow = lax.broadcasted_iota(jnp.int32, (cols, cols), 0)
        wcol = lax.broadcasted_iota(jnp.int32, (cols, cols), 1)
        weave = jnp.where(
            wrow == lax.rem(wcol, ps) * POOL + lax.div(wcol, ps), 1.0, 0.0
        ).astype(BF16)
        grow[0] = y[:cols]
        grow[1] = y[(rows - 1) * cols :]
        for i in range(1, rows - 1):
            gout[i] = mm(weave, y[i * cols : (i + 1) * cols].astype(BF16)).astype(BF16)

        wait(pg_cols)
        halves = []
        for side in range(2):
            at_end = (half - 1, 0)[side]
            cells = [pgmid[side, p].astype(F32)[at_end : at_end + 1] for p in range(pr)]
            cells = jnp.where(line < POOL, cells[0], cells[1])
            halves.append(column_taps(cells * colhalo[1, side, 0])[::-1])
        fixes = column_terms(
            halves[0],
            halves[1],
            [cw[a, 2] for a in range(3)] + [cw[a, 0] for a in range(3)],
            NT,
        )
        tile_row = lax.broadcasted_iota(jnp.int32, (16, chan), 0)
        for i in range(1, rows - 1):
            for side, cut, cell in ((0, slice(0, 16), 0), (1, slice(cols - 16, cols), 15)):
                gout[i, cut, :] = (
                    gout[i, cut, :].astype(F32)
                    + jnp.where(tile_row == cell, fixes[side][i : i + 1], 0.0)
                ).astype(BF16)
        wait(pg_rows)
        for k, pick, pole in ((0, rows - 1, 0), (1, 0, lat_n - 1)):
            there = jnp.where(lat == pole, 0.0, 1.0)
            pg = pgrow[k].astype(F32)
            slope = dslhalo[k].astype(F32)
            slabs = [pg * slope[t * ps : (t + 1) * ps] for t in range(POOL)]
            for t in range(POOL):
                ch[k, (t + 1) * ps : (t + 2) * ps, :] = slabs[t].astype(BF16)
            row_slabs(
                ch,
                k,
                slabs[0],
                slabs[POOL - 1],
                pgcor[0, k].astype(F32)[half - 1 : half]
                * colhalo[1, 0, 1 + k, pick : pick + 1, :],
                pgcor[1, k].astype(F32)[0:1] * colhalo[1, 1, 1 + k, pick : pick + 1, :],
            )
            lhs = jnp.concatenate(
                [ch[k, (2 - b) * ps : (2 - b) * ps + cols, :] for b in range(3)], axis=1
            )
            a = 2 - 2 * k
            y = mm(lhs, jnp.concatenate([cw[a, b] for b in range(3)], axis=1), NT)
            i = k * (rows - 1)
            y = grow[k] + y * there
            first_slab = y[:ps] + jnp.where(edge == 0, fixes[0][i : i + 1], 0.0)
            last_slab = y[cols - ps :] + jnp.where(edge == ps - 1, fixes[1][i : i + 1], 0.0)
            y = jnp.concatenate([first_slab, y[ps : cols - ps], last_slab], axis=0)
            gout[i] = mm(weave, y.astype(BF16)).astype(BF16)

    return kernel


def store_kernel(att, gout, attended, out_grad, sem):
    copies = [
        pltpu.make_async_copy(gout, out_grad, sem.at[0]),
        pltpu.make_async_copy(att, attended, sem.at[1]),
    ]
    for copy in copies:
        copy.start()
    for copy in copies:
        copy.wait()


def solution(mesh):
    lon_n, lat_n = mesh.shape["lon"], mesh.shape["lat"]

    def on_device(field, conv_w, wq, wk, wv, query_rows, attended_grad):
        rows, cols, chan = field.shape
        width = wq.shape[1]
        pr, ps = rows // POOL, cols // POOL
        keys = pr * ps
        chips = lon_n // 2
        hq = (width // HEAD_DIM) * ps
        slab_rows = (POOL + 2) * ps
        any_spec = pl.BlockSpec(memory_space=pl.ANY)
        vmem = pl.BlockSpec(memory_space=pltpu.VMEM)
        att, gout = pl.pallas_call(
            make_kernel(lon_n, lat_n, rows, cols, chan, width),
            out_shape=(
                pltpu.VMEM(attended_grad.shape, BF16),
                pltpu.VMEM(field.shape, BF16),
            ),
            in_specs=[any_spec] * 5 + [vmem, any_spec],
            out_specs=(vmem, vmem),
            scratch_shapes=[
                pltpu.VMEM((rows, cols, chan), BF16),
                pltpu.VMEM((rows + 2, slab_rows, chan), BF16),
                pltpu.VMEM((2, slab_rows, chan), BF16),
                pltpu.VMEM((rows + 2, slab_rows, chan), BF16),
                pltpu.VMEM((2, slab_rows, chan), BF16),
                pltpu.VMEM((3, 3, chan, chan), BF16),
                pltpu.VMEM((chan, width), BF16),
                pltpu.VMEM((chan, width), BF16),
                pltpu.VMEM((chan, width), BF16),
                pltpu.VMEM((2, ps, width), BF16),
                pltpu.VMEM((rows * cols, chan), F32),
                pltpu.VMEM((2, rows, chan), F32),
                pltpu.VMEM((2, cols, chan), F32),
                pltpu.VMEM((rows * cols, chan), F32),
                pltpu.VMEM((chips, keys, chan), BF16),
                pltpu.VMEM((2, ps, chan), BF16),
                pltpu.VMEM((chan, chips * keys), BF16),
                pltpu.VMEM((chips * keys, 2 * hq), F32),
                pltpu.VMEM((chips * keys, 2 * hq), F32),
                pltpu.VMEM((chips * keys, 4 * hq), BF16),
                pltpu.VMEM((chan, 4 * hq), BF16),
                pltpu.VMEM((4 * hq, chan), BF16),
                pltpu.VMEM((chips, keys, chan), BF16),
                pltpu.VMEM((chips, keys, chan), BF16),
                pltpu.VMEM((2, 8, 2 * hq), F32),
                pltpu.VMEM((2, ps, width + chan), F32),
                pltpu.VMEM((2, 2, rows, chan), F32),
                pltpu.VMEM((2, 2, 3, rows, chan), F32),
                pltpu.VMEM((2, cols, chan), BF16),
                pltpu.VMEM((2, cols, chan), BF16),
                pltpu.VMEM((pr, ps, chan), BF16),
                pltpu.VMEM((2, pr, ps // 2, chan), BF16),
                pltpu.VMEM((2, 2, ps // 2, chan), BF16),
                pltpu.VMEM((2, ps, chan), BF16),
                pltpu.SemaphoreType.DMA((6,)),
                pltpu.SemaphoreType.DMA((48,)),
                pltpu.SemaphoreType.DMA((48,)),
            ],
            compiler_params=pltpu.CompilerParams(
                collective_id=0, has_side_effects=True, vmem_limit_bytes=55 * 1024 * 1024
            ),
        )(field, conv_w, wq, wk, wv, query_rows, attended_grad)
        return pl.pallas_call(
            store_kernel,
            out_shape=(
                jax.ShapeDtypeStruct(attended_grad.shape, BF16),
                jax.ShapeDtypeStruct(field.shape, BF16),
            ),
            in_specs=[vmem] * 2,
            out_specs=(any_spec, any_spec),
            scratch_shapes=[pltpu.SemaphoreType.DMA((2,))],
        )(att, gout)

    return jax.shard_map(
        on_device,
        mesh=mesh,
        in_specs=(
            P("lat", "lon", None),
            P(),
            P(),
            P(),
            P(),
            P("lat", "lon", None),
            P("lat", "lon", None),
        ),
        out_specs=(P("lat", "lon", None), P("lat", "lon", None)),
        check_vma=False,
    )
```

time: 46.9 us -> 48.9 us (1.043)
  local copies, waits for them, and re-layouts: 0.01 us -> 1.41 us
  Pallas kernels: 45.5 us -> 46 us
    unnamed x2 -> x4, local copies, waits for them, and re-layouts: 0.01 us -> 1.41 us
    pallas_call x1, Pallas kernels: 43.4 us -> 44.1 us  [on_device(): pl.pallas_call(make_kernel(lon_n, lat_n, rows, cols, chan, width), out_sh...]
where the time goes in v3:
time: 48.9 us; the launch traced here: 48.7 us
  Pallas kernels  46 us (94%)
  local copies, waits for them, and re-layouts  1.41 us (3%)
  between operations  1.3 us (3%)
    pallas_call x1, Pallas kernels, on_device(): pl.pallas_call(make_kernel(lon_n, lat_n, rows, cols, chan, width), out_sh...  44.1 us
    pallas_call x1, Pallas kernels, on_device(): pl.pallas_call(store_kernel, out_shape=(jax.ShapeDtypeStruct(attended_gra...  1.9 us
    unnamed x4, local copies, waits for them, and re-layouts  1.41 us

profile of v3, /device:TPU:1, one launch (start us, length us, event | category | flops | bytes accessed | tf_op | source)
XLA Modules:
  0.0 48.7 jit_solution(6695925146422539512)
XLA Ops:
  1.3 44.1 %shard_map.86 = (bf16[1,32,1024]{2,1,0:T(8,128)(2,1)S(1)}, bf16[8,128,256]{2,1,0:T(8,128)(2,1)S(1)}) custom-call(bf16[8,128,256]{2,1,0:T(8,128)(2,1)} %field.1, bf16[3,3,256,256]{3,2,1,0:T(8,128)(2,1)} %conv_w.1, bf16[256,1024]{1,0:T(8,128)(2,1)} %wq_h.1, bf16[256,1024]{1,0:T(8,128)(2,1)} %wk_h.1, bf16[256,1024]{1,0:T(8,128)(2,1)} %wv_h.1, ...), custom_call_target="tpu_custom_call" | custom-call | tf_op jit(solution)/shard_map/pallas_call | solution.py:515
  45.4 0.0 copy-start
  45.4 0.8 %copy-done = bf16[8,128,256]{2,1,0:T(8,128)(2,1)} copy-done((bf16[8,128,256]{2,1,0:T(8,128)(2,1)}, bf16[8,128,256]{2,1,0:T(8,128)(2,1)S(1)}, u32[]{:S(2)}) %copy-start) | copy-done | bytes 524312
  46.2 0.0 copy-start.1
  46.2 0.6 %copy-done.1 = bf16[1,32,1024]{2,1,0:T(8,128)(2,1)} copy-done((bf16[1,32,1024]{2,1,0:T(8,128)(2,1)}, bf16[1,32,1024]{2,1,0:T(8,128)(2,1)S(1)}, u32[]{:S(2)}) %copy-start.1) | copy-done | bytes 65560
  46.8 1.9 %shard_map.87 = (bf16[1,32,1024]{2,1,0:T(8,128)(2,1)}, bf16[8,128,256]{2,1,0:T(8,128)(2,1)}) custom-call(bf16[1,32,1024]{2,1,0:T(8,128)(2,1)} %copy-done.1, bf16[8,128,256]{2,1,0:T(8,128)(2,1)} %copy-done), custom_call_target="tpu_custom_call" | custom-call | tf_op jit(solution)/shard_map/pallas_call | solution.py:566
Async XLA Ops:
  45.4 0.8 %copy-start = (bf16[8,128,256]{2,1,0:T(8,128)(2,1)}, bf16[8,128,256]{2,1,0:T(8,128)(2,1)S(1)}, u32[]{:S(2)}) copy-start(bf16[8,128,256]{2,1,0:T(8,128)(2,1)S(1)} %get-tuple-element.5.gout) | copy-start | bytes 1572868
  46.2 0.6 %copy-start.1 = (bf16[1,32,1024]{2,1,0:T(8,128)(2,1)}, bf16[1,32,1024]{2,1,0:T(8,128)(2,1)S(1)}, u32[]{:S(2)}) copy-start(bf16[1,32,1024]{2,1,0:T(8,128)(2,1)S(1)} %get-tuple-element.4.att) | copy-start | bytes 196612

commit v4 on v3

--- a/solution.py
+++ b/solution.py
@@ -54,7 +54,6 @@
     gq = group * ps
     slab_rows = (POOL + 2) * ps
     chips = lon_n // 2
-    half = ps // 2
     slot_shift = list(range(0, chips, 2)) + list(range(1, chips, 2))
     split = chips // 2
     halo = [
@@ -68,7 +67,7 @@
         attended, gout,
         xr, xs, xh, cg, ch, cw, wq, wk, wv, ag,
         cout, ccol, grow, dsl, nall, chosen, ntr, ex, dpr, pt, utb, gall, part, recv,
-        stat, joined, colmsg, colhalo, dslrow, dslhalo, pgb, pgmid, pgcor, pgrow,
+        stat, joined, colmsg, colhalo, colend, dslrow, dslhalo, pgb, pgcell, pgmid, pgend, pgrow,
         load_sem, send_sem, recv_sem,
     ):
         lon = lax.axis_index("lon")
@@ -120,10 +119,17 @@
         start(loads[1:])
 
         def columns(phase):
-            return [
-                remote(colmsg.at[phase, side], colhalo.at[phase, side, place], at(dlon, dlat))
-                for side, place, dlon, dlat in halo
-            ]
+            mids, ends = [], []
+            for side, place, dlon, dlat in halo:
+                if place == 0:
+                    src, dst = colmsg.at[phase, side], colhalo.at[phase, side]
+                    mids.append(remote(src, dst, at(dlon, dlat)))
+                else:
+                    cell = pl.ds(rows - 1 if place == 1 else 0, 1)
+                    src = colmsg.at[phase, side, cell]
+                    dst = colend.at[phase, side, place - 1, pl.ds(0, 1)]
+                    ends.append(remote(src, dst, at(dlon, dlat)))
+            return mids, ends
 
         prow = lax.broadcasted_iota(jnp.int32, (slab_rows, cols), 0)
         pcol = lax.broadcasted_iota(jnp.int32, (slab_rows, cols), 1)
@@ -143,9 +149,9 @@
             remote(xs.at[1, mid], xh.at[1, mid], at(0, -1)),
             remote(xs.at[rows, mid], xh.at[0, mid], at(0, 1)),
         ]
-        field_cols = columns(0)
+        field_cols, field_ends = columns(0)
         grads = remote(ag_h.at[0], ag.at[1], sibling)
-        start(field_rows + field_cols + [grads])
+        start(field_rows + field_cols + field_ends + [grads])
 
         xs[0] = jnp.zeros((slab_rows, chan), BF16)
         xs[rows + 1] = jnp.zeros((slab_rows, chan), BF16)
@@ -210,8 +216,8 @@
 
         wait(field_cols)
         fixes = column_terms(
-            column_taps(colhalo[0, 0, 0]),
-            column_taps(colhalo[0, 1, 0]),
+            column_taps(colhalo[0, 0]),
+            column_taps(colhalo[0, 1]),
             [cw[a, 0] for a in range(3)] + [cw[a, 2] for a in range(3)],
             NN,
         )
@@ -230,16 +236,16 @@
         for i in range(rows):
             cout[i * cols : i * cols + 1, :] = ccol[0, i : i + 1, :]
             cout[(i + 1) * cols - 1 : (i + 1) * cols, :] = ccol[1, i : i + 1, :]
-        wait(field_rows)
-        for k, pick, pole in ((0, rows - 1, 0), (1, 0, lat_n - 1)):
+        wait(field_rows + field_ends)
+        for k, pole in ((0, 0), (1, lat_n - 1)):
             there = jnp.where(lat == pole, 0.0, 1.0)
             row_slabs(
                 xh,
                 k,
                 xh[k, ps : 2 * ps, :].astype(F32),
                 xh[k, POOL * ps : (POOL + 1) * ps, :].astype(F32),
-                colhalo[0, 0, 1 + k, pick : pick + 1, :],
-                colhalo[0, 1, 1 + k, pick : pick + 1, :],
+                colend[0, 0, k, 0:1, :],
+                colend[0, 1, k, 0:1, :],
             )
             lhs = jnp.concatenate([xh[k, b * ps : b * ps + cols, :] for b in range(3)], axis=1)
             fix = mm(lhs, cw[2 * k].reshape(3 * chan, chan)) * there
@@ -283,73 +289,54 @@
                 dslrow[1] = d.astype(BF16)
         ident = eye(chan)
 
-        blk = chan
-        half_keys = split * keys
-
-        def score(part_at):
-            r0 = part_at * half_keys
-            nv = nall[part_at * split : (part_at + 1) * split].reshape(half_keys, chan)
-            for h0 in range(0, 2 * hq, blk):
-                s = mm(nv, gall[2 * hq + h0 : 2 * hq + h0 + blk, :], NT)
-                top = s.max(axis=0, keepdims=True)
-                e = jnp.exp(s - top)
-                dp = mm(nv, gall[h0 : h0 + blk, :], NT)
-                ex[r0 : r0 + half_keys, h0 : h0 + blk] = e
-                dpr[r0 : r0 + half_keys, h0 : h0 + blk] = dp
-                k = 3 * part_at
-                stat[0, k : k + 1, h0 : h0 + blk] = top
-                stat[0, k + 1 : k + 2, h0 : h0 + blk] = e.sum(axis=0, keepdims=True)
-                stat[0, k + 2 : k + 3, h0 : h0 + blk] = (e * dp).sum(axis=0, keepdims=True)
-            return nv
-
-        wait(gathers[: split - 1])
-        score(0)
-        wait(gathers[split - 1 :])
-        score(1)
-        stats = remote(stat.at[0], stat.at[1], sibling)
-        stats.start()
+        wait(gathers)
         slope_rows = [
             remote(dslrow.at[0], dslhalo.at[1], at(0, -1)),
             remote(dslrow.at[1], dslhalo.at[0], at(0, 1)),
         ]
-        slope_cols = columns(1)
-        start(slope_rows + slope_cols)
-        ntr[...] = mm(ident, nall[...].reshape(chips * keys, chan), NT).astype(BF16)
+        slope_cols, slope_ends = columns(1)
+        start(slope_rows + slope_cols + slope_ends)
+        blk = chan
+        nv = nall[...].reshape(chips * keys, chan)
+        for h0 in range(0, 2 * hq, blk):
+            s = mm(nv, gall[2 * hq + h0 : 2 * hq + h0 + blk, :], NT)
+            top = s.max(axis=0, keepdims=True)
+            e = jnp.exp(s - top)
+            dp = mm(nv, gall[h0 : h0 + blk, :], NT)
+            ex[:, h0 : h0 + blk] = e
+            dpr[:, h0 : h0 + blk] = dp
+            stat[0, 0:1, h0 : h0 + blk] = top
+            stat[0, 1:2, h0 : h0 + blk] = e.sum(axis=0, keepdims=True)
+            stat[0, 2:3, h0 : h0 + blk] = (e * dp).sum(axis=0, keepdims=True)
+        stats = remote(stat.at[0], stat.at[1], sibling)
+        stats.start()
+        ntr[...] = mm(ident, nv, NT).astype(BF16)
         stats.wait()
         scale = {}
         for h0 in range(0, 2 * hq, blk):
             o0 = (h0 + hq) % (2 * hq)
-            tops, sizes, dots = (
-                [
-                    stat[who, 3 * q + k : 3 * q + k + 1, c0 : c0 + blk]
-                    for who, c0 in ((0, h0), (1, o0))
-                    for q in range(2)
-                ]
-                for k in range(3)
-            )
-            peak = jnp.maximum(jnp.maximum(tops[0], tops[1]), jnp.maximum(tops[2], tops[3]))
-            f = [jnp.exp(t - peak) for t in tops]
-            inv = 1.0 / sum(a * b for a, b in zip(sizes, f))
-            delta = sum(a * b for a, b in zip(dots, f)) * inv
-            scale[h0] = (f[0] * inv, f[1] * inv, delta)
+            top, size, dot = (stat[0, k : k + 1, h0 : h0 + blk] for k in range(3))
+            top2, size2, dot2 = (stat[1, k : k + 1, o0 : o0 + blk] for k in range(3))
+            peak = jnp.maximum(top, top2)
+            f, f2 = jnp.exp(top - peak), jnp.exp(top2 - peak)
+            inv = 1.0 / (size * f + size2 * f2)
+            scale[h0] = (f * inv, (dot * f + dot2 * f2) * inv)
 
         scatters = []
         own = None
-        for part_at in (1, 0):
-            r0 = part_at * half_keys
-            for h0 in range(0, 2 * hq, blk):
-                prob = ex[r0 : r0 + half_keys, h0 : h0 + blk] * scale[h0][part_at]
-                pt[r0 : r0 + half_keys, h0 : h0 + blk] = prob.astype(BF16)
-                pt[r0 : r0 + half_keys, 2 * hq + h0 : 2 * hq + h0 + blk] = (
-                    prob * (dpr[r0 : r0 + half_keys, h0 : h0 + blk] - scale[h0][2])
-                ).astype(BF16)
-            y = mm(pt[r0 : r0 + half_keys, :], gall[...])
-            if part_at == 0:
+        for h0 in range(0, 2 * hq, blk):
+            prob = ex[:, h0 : h0 + blk] * scale[h0][0]
+            pt[:, h0 : h0 + blk] = prob.astype(BF16)
+            pt[:, 2 * hq + h0 : 2 * hq + h0 + blk] = (
+                prob * (dpr[:, h0 : h0 + blk] - scale[h0][1])
+            ).astype(BF16)
+        pair = split // 2
+        for k0 in (split, 0, split + pair, pair):
+            y = mm(pt[k0 * keys : (k0 + pair) * keys, :], gall[...])
+            if k0 == 0:
                 own = y[:keys]
-            part[part_at * split : (part_at + 1) * split] = y.astype(BF16).reshape(
-                split, keys, chan
-            )
-            for k in range(max(part_at * split, 1), (part_at + 1) * split):
+            part[k0 : k0 + pair] = y.astype(BF16).reshape(pair, keys, chan)
+            for k in range(max(k0, 1), k0 + pair):
                 scatters.append(remote(part.at[k], recv.at[k], at(-2 * slot_shift[k], 0)))
                 scatters[-1].start()
 
@@ -389,7 +376,7 @@
         total = own + jnp.concatenate(
             [jnp.where(first, qfeat, zero), jnp.where(first, zero, qfeat)], axis=0
         )
-        wait(slope_rows + slope_cols)
+        wait(slope_rows + slope_cols + slope_ends)
         wait(scatters)
         total = total + recv[1:].astype(F32).sum(axis=0)
         pgrad = inv_std * (
@@ -398,20 +385,24 @@
             - standard * (total * standard).mean(-1, keepdims=True)
         )
         pgb[...] = pgrad.astype(BF16).reshape(pr, ps, chan)
-        sides = (pl.ds(ps - half, half), pl.ds(0, half))
+        for side in range(2):
+            for p in range(pr):
+                r = p * ps + (ps - 1, 0)[side]
+                pgcell[side * pr + p : side * pr + p + 1, :] = pgrad[r : r + 1]
         pg_rows = [
             remote(pgb.at[0], pgrow.at[1], at(0, -1)),
             remote(pgb.at[pr - 1], pgrow.at[0], at(0, 1)),
         ]
-        pg_cols = []
+        pg_cols, pg_ends = [], []
         for side, place, dlon, dlat in halo:
             if place == 0:
-                src, dst = pgb.at[:, sides[side]], pgmid.at[side]
+                src, dst = pgcell.at[pl.ds(side * pr, pr)], pgmid.at[side, pl.ds(0, pr)]
+                pg_cols.append(remote(src, dst, at(dlon, dlat)))
             else:
-                src = pgb.at[pr - 1 if place == 1 else 0, sides[side]]
-                dst = pgcor.at[side, place - 1]
-            pg_cols.append(remote(src, dst, at(dlon, dlat)))
-        start(pg_rows + pg_cols)
+                src = pgcell.at[pl.ds(side * pr + (pr - 1 if place == 1 else 0), 1)]
+                dst = pgend.at[side, place - 1, pl.ds(0, 1)]
+                pg_ends.append(remote(src, dst, at(dlon, dlat)))
+        start(pg_rows + pg_ends + pg_cols)
 
         cg[0] = jnp.zeros((slab_rows, chan), BF16)
         cg[rows + 1] = jnp.zeros((slab_rows, chan), BF16)
@@ -439,10 +430,8 @@
         wait(pg_cols)
         halves = []
         for side in range(2):
-            at_end = (half - 1, 0)[side]
-            cells = [pgmid[side, p].astype(F32)[at_end : at_end + 1] for p in range(pr)]
-            cells = jnp.where(line < POOL, cells[0], cells[1])
-            halves.append(column_taps(cells * colhalo[1, side, 0])[::-1])
+            cells = jnp.where(line < POOL, pgmid[side, 0:1, :], pgmid[side, 1:2, :])
+            halves.append(column_taps(cells * colhalo[1, side])[::-1])
         fixes = column_terms(
             halves[0],
             halves[1],
@@ -456,8 +445,8 @@
                     gout[i, cut, :].astype(F32)
                     + jnp.where(tile_row == cell, fixes[side][i : i + 1], 0.0)
                 ).astype(BF16)
-        wait(pg_rows)
-        for k, pick, pole in ((0, rows - 1, 0), (1, 0, lat_n - 1)):
+        wait(pg_rows + pg_ends)
+        for k, pole in ((0, 0), (1, lat_n - 1)):
             there = jnp.where(lat == pole, 0.0, 1.0)
             pg = pgrow[k].astype(F32)
             slope = dslhalo[k].astype(F32)
@@ -469,9 +458,8 @@
                 k,
                 slabs[0],
                 slabs[POOL - 1],
-                pgcor[0, k].astype(F32)[half - 1 : half]
-                * colhalo[1, 0, 1 + k, pick : pick + 1, :],
-                pgcor[1, k].astype(F32)[0:1] * colhalo[1, 1, 1 + k, pick : pick + 1, :],
+                pgend[0, k, 0:1, :] * colend[1, 0, k, 0:1, :],
+                pgend[1, k, 0:1, :] * colend[1, 1, k, 0:1, :],
             )
             lhs = jnp.concatenate(
                 [ch[k, (2 - b) * ps : (2 - b) * ps + cols, :] for b in range(3)], axis=1
@@ -548,12 +536,14 @@
                 pltpu.VMEM((2, 8, 2 * hq), F32),
                 pltpu.VMEM((2, ps, width + chan), F32),
                 pltpu.VMEM((2, 2, rows, chan), F32),
-                pltpu.VMEM((2, 2, 3, rows, chan), F32),
+                pltpu.VMEM((2, 2, rows, chan), F32),
+                pltpu.VMEM((2, 2, 2, 8, chan), F32),
                 pltpu.VMEM((2, cols, chan), BF16),
                 pltpu.VMEM((2, cols, chan), BF16),
                 pltpu.VMEM((pr, ps, chan), BF16),
-                pltpu.VMEM((2, pr, ps // 2, chan), BF16),
-                pltpu.VMEM((2, 2, ps // 2, chan), BF16),
+                pltpu.VMEM((8, chan), F32),
+                pltpu.VMEM((2, 8, chan), F32),
+                pltpu.VMEM((2, 2, 8, chan), F32),
                 pltpu.VMEM((2, ps, chan), BF16),
                 pltpu.SemaphoreType.DMA((6,)),
                 pltpu.SemaphoreType.DMA((48,)),
@@ -572,6 +562,7 @@
             in_specs=[vmem] * 2,
             out_specs=(any_spec, any_spec),
             scratch_shapes=[pltpu.SemaphoreType.DMA((2,))],
+            compiler_params=pltpu.CompilerParams(vmem_limit_bytes=4 * 1024 * 1024),
         )(att, gout)
 
     return jax.shard_map(

time: 48.9 us -> 44.3 us (0.906)
  Pallas kernels: 46 us -> 42.9 us
  local copies, waits for them, and re-layouts: 1.41 us -> 0 us
    pallas_call x1, Pallas kernels: 44.1 us -> 42.1 us  [on_device(): pl.pallas_call(make_kernel(lon_n, lat_n, rows, cols, chan, width), out_sh...]
    unnamed x4 -> x0, local copies, waits for them, and re-layouts: 1.41 us -> none
    pallas_call x1, Pallas kernels: 1.9 us -> 0.82 us  [on_device(): pl.pallas_call(store_kernel, out_shape=(jax.ShapeDtypeStruct(attended_gra...]
where the time goes in v4:
time: 44.3 us; the launch traced here: 44.2 us
  Pallas kernels  42.9 us (97%)
  between operations  1.29 us (3%)
    pallas_call x1, Pallas kernels, on_device(): pl.pallas_call(make_kernel(lon_n, lat_n, rows, cols, chan, width), out_sh...  42.1 us

profile of v4, /device:TPU:1, one launch (start us, length us, event | category | flops | bytes accessed | tf_op | source)
XLA Modules:
  0.0 44.2 jit_solution(13163995817372239058)
XLA Ops:
  1.3 42.1 %shard_map.86 = (bf16[1,32,1024]{2,1,0:T(8,128)(2,1)S(1)}, bf16[8,128,256]{2,1,0:T(8,128)(2,1)S(1)}) custom-call(bf16[8,128,256]{2,1,0:T(8,128)(2,1)} %field.1, bf16[3,3,256,256]{3,2,1,0:T(8,128)(2,1)} %conv_w.1, bf16[256,1024]{1,0:T(8,128)(2,1)} %wq_h.1, bf16[256,1024]{1,0:T(8,128)(2,1)} %wk_h.1, bf16[256,1024]{1,0:T(8,128)(2,1)} %wv_h.1, ...), custom_call_target="tpu_custom_call" | custom-call | tf_op jit(solution)/shard_map/pallas_call | solution.py:503
  43.4 0.8 %shard_map.87 = (bf16[1,32,1024]{2,1,0:T(8,128)(2,1)}, bf16[8,128,256]{2,1,0:T(8,128)(2,1)}) custom-call(bf16[1,32,1024]{2,1,0:T(8,128)(2,1)S(1)} %get-tuple-element.4.att, bf16[8,128,256]{2,1,0:T(8,128)(2,1)S(1)} %get-tuple-element.5.gout), custom_call_target="tpu_custom_call" | custom-call | tf_op jit(solution)/shard_map/pallas_call | solution.py:556

commit v5 on v4

--- a/solution.py
+++ b/solution.py
@@ -54,7 +54,7 @@
     gq = group * ps
     slab_rows = (POOL + 2) * ps
     chips = lon_n // 2
-    slot_shift = list(range(0, chips, 2)) + list(range(1, chips, 2))
+    slot_shift = sorted(range(chips), key=lambda e: (e % 2, min(e, chips - e)))
     split = chips // 2
     halo = [
         (0, 0, 1, 0), (1, 0, -1, 0),
@@ -65,7 +65,7 @@
     def kernel(
         field, conv_w, wq_h, wk_h, wv_h, qrow, ag_h,
         attended, gout,
-        xr, xs, xh, cg, ch, cw, wq, wk, wv, ag,
+        xr, xs, xh, cg, cw, wq, wk, wv, ag,
         cout, ccol, grow, dsl, nall, chosen, ntr, ex, dpr, pt, utb, gall, part, recv,
         stat, joined, colmsg, colhalo, colend, dslrow, dslhalo, pgb, pgcell, pgmid, pgend, pgrow,
         load_sem, send_sem, recv_sem,
@@ -146,8 +146,8 @@
             colmsg[0, 1, i : i + 1, :] = xr[i, 0:16, :].astype(F32)[0:1]
         pl.semaphore_wait(barrier, len(friends))
         field_rows = [
-            remote(xs.at[1, mid], xh.at[1, mid], at(0, -1)),
-            remote(xs.at[rows, mid], xh.at[0, mid], at(0, 1)),
+            remote(xs.at[1, mid], xh.at[1], at(0, -1)),
+            remote(xs.at[rows, mid], xh.at[0], at(0, 1)),
         ]
         field_cols, field_ends = columns(0)
         grads = remote(ag_h.at[0], ag.at[1], sibling)
@@ -190,12 +190,14 @@
             y = mm(lhs, jnp.concatenate(weights, axis=axis), dims)
             return y[:rows], y[rows:]
 
-        def row_slabs(ref, k, first_slab, last_slab, left, right):
-            lo = pltpu.roll(last_slab, 1, 0)
-            hi = pltpu.roll(first_slab, ps - 1, 0)
-            ref[k, 0:ps, :] = jnp.where(edge == 0, left, lo).astype(BF16)
-            ref[k, slab_rows - ps : slab_rows, :] = jnp.where(edge == ps - 1, right, hi).astype(
-                BF16
+        def padded(slabs, left, right):
+            lo = jnp.where(edge == 0, left, pltpu.roll(slabs[POOL - 1], 1, 0))
+            hi = jnp.where(edge == ps - 1, right, pltpu.roll(slabs[0], ps - 1, 0))
+            return [slab.astype(BF16) for slab in [lo, *slabs, hi]]
+
+        def row_windows(slabs, shifts):
+            return jnp.concatenate(
+                [jnp.concatenate(slabs[b : b + POOL], axis=0) for b in shifts], axis=1
             )
 
         hrow = lax.div(lax.broadcasted_iota(jnp.int32, (gq, chan), 0), ps)
@@ -237,20 +239,16 @@
             cout[i * cols : i * cols + 1, :] = ccol[0, i : i + 1, :]
             cout[(i + 1) * cols - 1 : (i + 1) * cols, :] = ccol[1, i : i + 1, :]
         wait(field_rows + field_ends)
-        for k, pole in ((0, 0), (1, lat_n - 1)):
-            there = jnp.where(lat == pole, 0.0, 1.0)
-            row_slabs(
-                xh,
-                k,
-                xh[k, ps : 2 * ps, :].astype(F32),
-                xh[k, POOL * ps : (POOL + 1) * ps, :].astype(F32),
-                colend[0, 0, k, 0:1, :],
-                colend[0, 1, k, 0:1, :],
-            )
-            lhs = jnp.concatenate([xh[k, b * ps : b * ps + cols, :] for b in range(3)], axis=1)
-            fix = mm(lhs, cw[2 * k].reshape(3 * chan, chan)) * there
+        poles = [jnp.where(lat == pole, 0.0, 1.0) for pole in (0, lat_n - 1)]
+        lhs = []
+        for k in range(2):
+            slabs = [xh[k, t * ps : (t + 1) * ps, :].astype(F32) for t in range(POOL)]
+            slabs = padded(slabs, colend[0, 0, k, 0:1, :], colend[0, 1, k, 0:1, :])
+            lhs.append(row_windows(slabs, range(3)))
+        fix = [mm(lhs[k], cw[2 * k].reshape(3 * chan, chan)) * poles[k] for k in range(2)]
+        for k in range(2):
             i = k * (rows - 1)
-            v = cout[i * cols : (i + 1) * cols, :] + fix
+            v = cout[i * cols : (i + 1) * cols, :] + fix[k]
             cout[i * cols : (i + 1) * cols, :] = v
             p = k * (pr - 1)
             pooled[p] = pooled[p] + silu(v).reshape(POOL, ps, chan).sum(axis=0)
@@ -266,7 +264,7 @@
             remote(nall.at[0], nall.at[k], at(2 * slot_shift[k], 0)) for k in range(1, chips)
         ]
         picks = remote(chosen.at[0], chosen.at[1], sibling)
-        start([picks] + gathers[split - 1 :] + gathers[: split - 1])
+        start([picks] + gathers[: split - 2 : -1] + gathers[split - 2 :: -1])
 
         loads[4].wait()
         loads[5].wait()
@@ -331,7 +329,7 @@
                 prob * (dpr[:, h0 : h0 + blk] - scale[h0][1])
             ).astype(BF16)
         pair = split // 2
-        for k0 in (split, 0, split + pair, pair):
+        for k0 in (split + pair, pair, split, 0):
             y = mm(pt[k0 * keys : (k0 + pair) * keys, :], gall[...])
             if k0 == 0:
                 own = y[:keys]
@@ -412,9 +410,8 @@
             slabs = [
                 pg * dsl[i * cols + t * ps : i * cols + (t + 1) * ps, :] for t in range(POOL)
             ]
-            for t in range(POOL):
-                cg[1 + i, (t + 1) * ps : (t + 2) * ps, :] = slabs[t].astype(BF16)
-            row_slabs(cg, 1 + i, slabs[0], slabs[POOL - 1], 0.0, 0.0)
+            for t, slab in enumerate(padded(slabs, 0.0, 0.0)):
+                cg[1 + i, t * ps : (t + 1) * ps, :] = slab
         weights = jnp.concatenate([cw[a, b] for a in range(3) for b in range(3)], axis=1)
         y = mm(windows(cg, rows, cols, ps, True), weights, NT)
         wrow = lax.broadcasted_iota(jnp.int32, (cols, cols), 0)
@@ -439,6 +436,12 @@
             NT,
         )
         tile_row = lax.broadcasted_iota(jnp.int32, (16, chan), 0)
+        for k in range(2):
+            i = k * (rows - 1)
+            grow[k, 0:ps, :] = grow[k, 0:ps, :] + jnp.where(edge == 0, fixes[0][i : i + 1], 0.0)
+            grow[k, cols - ps : cols, :] = grow[k, cols - ps : cols, :] + jnp.where(
+                edge == ps - 1, fixes[1][i : i + 1], 0.0
+            )
         for i in range(1, rows - 1):
             for side, cut, cell in ((0, slice(0, 16), 0), (1, slice(cols - 16, cols), 15)):
                 gout[i, cut, :] = (
@@ -446,32 +449,24 @@
                     + jnp.where(tile_row == cell, fixes[side][i : i + 1], 0.0)
                 ).astype(BF16)
         wait(pg_rows + pg_ends)
-        for k, pole in ((0, 0), (1, lat_n - 1)):
-            there = jnp.where(lat == pole, 0.0, 1.0)
+        lhs = []
+        for k in range(2):
             pg = pgrow[k].astype(F32)
             slope = dslhalo[k].astype(F32)
             slabs = [pg * slope[t * ps : (t + 1) * ps] for t in range(POOL)]
-            for t in range(POOL):
-                ch[k, (t + 1) * ps : (t + 2) * ps, :] = slabs[t].astype(BF16)
-            row_slabs(
-                ch,
-                k,
-                slabs[0],
-                slabs[POOL - 1],
+            slabs = padded(
+                slabs,
                 pgend[0, k, 0:1, :] * colend[1, 0, k, 0:1, :],
                 pgend[1, k, 0:1, :] * colend[1, 1, k, 0:1, :],
             )
-            lhs = jnp.concatenate(
-                [ch[k, (2 - b) * ps : (2 - b) * ps + cols, :] for b in range(3)], axis=1
-            )
-            a = 2 - 2 * k
-            y = mm(lhs, jnp.concatenate([cw[a, b] for b in range(3)], axis=1), NT)
-            i = k * (rows - 1)
-            y = grow[k] + y * there
-            first_slab = y[:ps] + jnp.where(edge == 0, fixes[0][i : i + 1], 0.0)
-            last_slab = y[cols - ps :] + jnp.where(edge == ps - 1, fixes[1][i : i + 1], 0.0)
-            y = jnp.concatenate([first_slab, y[ps : cols - ps], last_slab], axis=0)
-            gout[i] = mm(weave, y.astype(BF16)).astype(BF16)
+            lhs.append(row_windows(slabs, (2, 1, 0)))
+        y = [
+            mm(lhs[k], jnp.concatenate([cw[2 - 2 * k, b] for b in range(3)], axis=1), NT)
+            for k in range(2)
+        ]
+        for k in range(2):
+            out = grow[k] + y[k] * poles[k]
+            gout[k * (rows - 1)] = mm(weave, out.astype(BF16)).astype(BF16)
 
     return kernel
 
@@ -511,9 +506,8 @@
             scratch_shapes=[
                 pltpu.VMEM((rows, cols, chan), BF16),
                 pltpu.VMEM((rows + 2, slab_rows, chan), BF16),
-                pltpu.VMEM((2, slab_rows, chan), BF16),
+                pltpu.VMEM((2, cols, chan), BF16),
                 pltpu.VMEM((rows + 2, slab_rows, chan), BF16),
-                pltpu.VMEM((2, slab_rows, chan), BF16),
                 pltpu.VMEM((3, 3, chan, chan), BF16),
                 pltpu.VMEM((chan, width), BF16),
                 pltpu.VMEM((chan, width), BF16),

time: 44.3 us -> 43.9 us (level)
    pallas_call x1, Pallas kernels: 42.1 us -> 41.6 us  [on_device(): pl.pallas_call(make_kernel(lon_n, lat_n, rows, cols, chan, width), out_sh...]
where the time goes in v5:
time: 43.9 us; the launch traced here: 43.7 us
  Pallas kernels  42.5 us (97%)
  between operations  1.29 us (3%)
    pallas_call x1, Pallas kernels, on_device(): pl.pallas_call(make_kernel(lon_n, lat_n, rows, cols, chan, width), out_sh...  41.6 us

profile of v5, /device:TPU:1, one launch (start us, length us, event | category | flops | bytes accessed | tf_op | source)
XLA Modules:
  0.0 43.7 jit_solution(6420220560413592804)
XLA Ops:
  1.3 41.6 %shard_map.86 = (bf16[1,32,1024]{2,1,0:T(8,128)(2,1)S(1)}, bf16[8,128,256]{2,1,0:T(8,128)(2,1)S(1)}) custom-call(bf16[8,128,256]{2,1,0:T(8,128)(2,1)} %field.1, bf16[3,3,256,256]{3,2,1,0:T(8,128)(2,1)} %conv_w.1, bf16[256,1024]{1,0:T(8,128)(2,1)} %wq_h.1, bf16[256,1024]{1,0:T(8,128)(2,1)} %wk_h.1, bf16[256,1024]{1,0:T(8,128)(2,1)} %wv_h.1, ...), custom_call_target="tpu_custom_call" | custom-call | tf_op jit(solution)/shard_map/pallas_call | solution.py:498
  42.9 0.8 %shard_map.87 = (bf16[1,32,1024]{2,1,0:T(8,128)(2,1)}, bf16[8,128,256]{2,1,0:T(8,128)(2,1)}) custom-call(bf16[1,32,1024]{2,1,0:T(8,128)(2,1)S(1)} %get-tuple-element.4.att, bf16[8,128,256]{2,1,0:T(8,128)(2,1)S(1)} %get-tuple-element.5.gout), custom_call_target="tpu_custom_call" | custom-call | tf_op jit(solution)/shard_map/pallas_call | solution.py:550

commit v6 on v5

--- a/solution.py
+++ b/solution.py
@@ -151,7 +151,7 @@
         ]
         field_cols, field_ends = columns(0)
         grads = remote(ag_h.at[0], ag.at[1], sibling)
-        start(field_rows + field_cols + field_ends + [grads])
+        start(field_ends + field_rows + field_cols)
 
         xs[0] = jnp.zeros((slab_rows, chan), BF16)
         xs[rows + 1] = jnp.zeros((slab_rows, chan), BF16)
@@ -238,6 +238,7 @@
         for i in range(rows):
             cout[i * cols : i * cols + 1, :] = ccol[0, i : i + 1, :]
             cout[(i + 1) * cols - 1 : (i + 1) * cols, :] = ccol[1, i : i + 1, :]
+        grads.start()
         wait(field_rows + field_ends)
         poles = [jnp.where(lat == pole, 0.0, 1.0) for pole in (0, lat_n - 1)]
         lhs = []
@@ -374,8 +375,8 @@
         total = own + jnp.concatenate(
             [jnp.where(first, qfeat, zero), jnp.where(first, zero, qfeat)], axis=0
         )
+        wait(scatters)
         wait(slope_rows + slope_cols + slope_ends)
-        wait(scatters)
         total = total + recv[1:].astype(F32).sum(axis=0)
         pgrad = inv_std * (
             total
@@ -400,7 +401,7 @@
                 src = pgcell.at[pl.ds(side * pr + (pr - 1 if place == 1 else 0), 1)]
                 dst = pgend.at[side, place - 1, pl.ds(0, 1)]
                 pg_ends.append(remote(src, dst, at(dlon, dlat)))
-        start(pg_rows + pg_ends + pg_cols)
+        start(pg_ends + pg_rows + pg_cols)
 
         cg[0] = jnp.zeros((slab_rows, chan), BF16)
         cg[rows + 1] = jnp.zeros((slab_rows, chan), BF16)

time: 43.9 us -> 43.1 us (0.982)
  Pallas kernels: 42.5 us -> 41.7 us
    pallas_call x1, Pallas kernels: 41.6 us -> 40.9 us  [on_device(): pl.pallas_call(make_kernel(lon_n, lat_n, rows, cols, chan, width), out_sh...]
where the time goes in v6:
time: 43.1 us; the launch traced here: 43 us
  Pallas kernels  41.7 us (97%)
  between operations  1.29 us (3%)
    pallas_call x1, Pallas kernels, on_device(): pl.pallas_call(make_kernel(lon_n, lat_n, rows, cols, chan, width), out_sh...  40.9 us

profile of v6, /device:TPU:1, one launch (start us, length us, event | category | flops | bytes accessed | tf_op | source)
XLA Modules:
  0.0 43.0 jit_solution(6660887728926071769)
XLA Ops:
  1.3 40.9 %shard_map.86 = (bf16[1,32,1024]{2,1,0:T(8,128)(2,1)S(1)}, bf16[8,128,256]{2,1,0:T(8,128)(2,1)S(1)}) custom-call(bf16[8,128,256]{2,1,0:T(8,128)(2,1)} %field.1, bf16[3,3,256,256]{3,2,1,0:T(8,128)(2,1)} %conv_w.1, bf16[256,1024]{1,0:T(8,128)(2,1)} %wq_h.1, bf16[256,1024]{1,0:T(8,128)(2,1)} %wk_h.1, bf16[256,1024]{1,0:T(8,128)(2,1)} %wv_h.1, ...), custom_call_target="tpu_custom_call" | custom-call | tf_op jit(solution)/shard_map/pallas_call | solution.py:499
  42.2 0.8 %shard_map.87 = (bf16[1,32,1024]{2,1,0:T(8,128)(2,1)}, bf16[8,128,256]{2,1,0:T(8,128)(2,1)}) custom-call(bf16[1,32,1024]{2,1,0:T(8,128)(2,1)S(1)} %get-tuple-element.4.att, bf16[8,128,256]{2,1,0:T(8,128)(2,1)S(1)} %get-tuple-element.5.gout), custom_call_target="tpu_custom_call" | custom-call | tf_op jit(solution)/shard_map/pallas_call | solution.py:551

commit v7 on v6

--- a/solution.py
+++ b/solution.py
@@ -295,7 +295,7 @@
         ]
         slope_cols, slope_ends = columns(1)
         start(slope_rows + slope_cols + slope_ends)
-        blk = chan
+        blk = 2 * chan
         nv = nall[...].reshape(chips * keys, chan)
         for h0 in range(0, 2 * hq, blk):
             s = mm(nv, gall[2 * hq + h0 : 2 * hq + h0 + blk, :], NT)
@@ -329,13 +329,12 @@
             pt[:, 2 * hq + h0 : 2 * hq + h0 + blk] = (
                 prob * (dpr[:, h0 : h0 + blk] - scale[h0][1])
             ).astype(BF16)
-        pair = split // 2
-        for k0 in (split + pair, pair, split, 0):
-            y = mm(pt[k0 * keys : (k0 + pair) * keys, :], gall[...])
+        for k0 in (split, 0):
+            y = mm(pt[k0 * keys : (k0 + split) * keys, :], gall[...])
             if k0 == 0:
                 own = y[:keys]
-            part[k0 : k0 + pair] = y.astype(BF16).reshape(pair, keys, chan)
-            for k in range(max(k0, 1), k0 + pair):
+            part[k0 : k0 + split] = y.astype(BF16).reshape(split, keys, chan)
+            for k in range(k0 + split - 1, max(k0, 1) - 1, -1):
                 scatters.append(remote(part.at[k], recv.at[k], at(-2 * slot_shift[k], 0)))
                 scatters[-1].start()
 

time: 43.1 us -> 42.8 us (level)
  no operation moved by 1% of the time
where the time goes in v7:
time: 42.8 us; the launch traced here: 42.7 us
  Pallas kernels  41.4 us (97%)
  between operations  1.29 us (3%)
    pallas_call x1, Pallas kernels, on_device(): pl.pallas_call(make_kernel(lon_n, lat_n, rows, cols, chan, width), out_sh...  40.6 us

profile of v7, /device:TPU:1, one launch (start us, length us, event | category | flops | bytes accessed | tf_op | source)
XLA Modules:
  0.0 42.7 jit_solution(17828093506602318974)
XLA Ops:
  1.3 40.6 %shard_map.86 = (bf16[1,32,1024]{2,1,0:T(8,128)(2,1)S(1)}, bf16[8,128,256]{2,1,0:T(8,128)(2,1)S(1)}) custom-call(bf16[8,128,256]{2,1,0:T(8,128)(2,1)} %field.1, bf16[3,3,256,256]{3,2,1,0:T(8,128)(2,1)} %conv_w.1, bf16[256,1024]{1,0:T(8,128)(2,1)} %wq_h.1, bf16[256,1024]{1,0:T(8,128)(2,1)} %wk_h.1, bf16[256,1024]{1,0:T(8,128)(2,1)} %wv_h.1, ...), custom_call_target="tpu_custom_call" | custom-call | tf_op jit(solution)/shard_map/pallas_call | solution.py:498
  41.9 0.8 %shard_map.87 = (bf16[1,32,1024]{2,1,0:T(8,128)(2,1)}, bf16[8,128,256]{2,1,0:T(8,128)(2,1)}) custom-call(bf16[1,32,1024]{2,1,0:T(8,128)(2,1)S(1)} %get-tuple-element.4.att, bf16[8,128,256]{2,1,0:T(8,128)(2,1)S(1)} %get-tuple-element.5.gout), custom_call_target="tpu_custom_call" | custom-call | tf_op jit(solution)/shard_map/pallas_call | solution.py:550
